TPU v7x, 128 devices: a whole 4x4x4 slice. The times are simulated.
128 devices in a mesh: section: 2 (over z_lo), fsdp: 16 (over z_hi, y, core), rep: 4 (over x).
Axes of the slice: x: 4, y: 4, z: 4 (z_hi: 2, z_lo: 2; z = z_hi * 2 + z_lo), core: 2. Of those that a mesh axis runs over, the one named last changes fastest.
Arguments:
- layer_input: bfloat16 [2, 4, 1024, 1024], P(None, 'rep', 'fsdp'), may hold values from -6 to 6
- cotangent: bfloat16 [2, 4, 1024, 1024], P(None, 'rep', 'fsdp'), may hold values from -6 to 6
- seq_lengths: int32 [2, 4, 4], P(None, 'rep'), may hold values from 0 to 1024, as said below
- norm_gains: bfloat16 [2, 2, 1024], P('section', None, 'fsdp'), may hold values from 0.099609375 to 1.8984375
- w_mix: bfloat16 [2, 1024, 4096], P('section', 'fsdp'), may hold values from -0.1875 to 0.1875
- w_step: bfloat16 [2, 1024, 24], P('section', 'fsdp'), may hold values from -0.1875 to 0.1875
- conv_kernel: bfloat16 [2, 4, 1792], P('section', None, 'fsdp'), may hold values from -3 to 3
- conv_bias: bfloat16 [2, 1792], P('section', 'fsdp'), may hold values from -3 to 3
- head_params: float32 [2, 3, 24], P('section'), may hold values from -13 to 1.5, as said below
- w_out: bfloat16 [2, 2048, 1024], P('section', 'fsdp'), may hold values from -0.25 to 0.25
- w_gate_up: bfloat16 [2, 1024, 4096], P('section', 'fsdp'), may hold values from -0.1875 to 0.1875
- w_down: bfloat16 [2, 2048, 1024], P('section', 'fsdp'), may hold values from -0.125 to 0.125
Outputs:
- activations: bfloat16 [2, 2, 4, 1024, 1024], P('section', None, 'rep', 'fsdp')
- input_grad: float32 [2, 2, 4, 1024, 1024], P('section', None, 'rep', 'fsdp')
- grad_norm_gains: float32 [2, 2, 1024], P('section', None, 'fsdp')
- grad_w_mix: float32 [2, 1024, 4096], P('section', 'fsdp')
- grad_w_step: float32 [2, 1024, 24], P('section', 'fsdp')
- grad_conv_kernel: float32 [2, 4, 1792], P('section', None, 'fsdp')
- grad_conv_bias: float32 [2, 1792], P('section', 'fsdp')
- grad_head_params: float32 [2, 3, 24], P('section')
- grad_w_out: float32 [2, 2048, 1024], P('section', 'fsdp')
- grad_w_gate_up: float32 [2, 1024, 4096], P('section', 'fsdp')
- grad_w_down: float32 [2, 2048, 1024], P('section', 'fsdp')
Inputs may be any that keep to these rules, and one draw needn't show every extreme that they name: `seq_lengths`: in each pack the sequences, each padded up to whole blocks of 64 tokens, take at most 1024 tokens together, and at least one slot is used; in each group one micro-batch holds a single sequence of 1024 tokens. `head_params`: row 2 (skip gains) lies in 0.5 to 1.5, row 1 (log rates) in -0.5 to 0.5.
All inputs are finite; a program needn't handle non-finite values.
Results may differ from a plain program's by a relative error of at most 0.025.
Values may be sent and summed in bfloat16 or wider, within the bound.
No kernel may reach another device: no remote copies, remote signals or barrier semaphores. Data moves between devices by JAX's collectives and lax.ppermute only.
A program may use at most 256 MiB of HBM per device.

v0:
```python
import jax
import jax.numpy as jnp
from jax import lax
from jax.sharding import PartitionSpec as P

QUERY_HEADS = 8
KEY_VALUE_HEADS = 2
HEAD_SIZE = 64
MIXER_HEADS = 24
MIXER_HEAD_SIZE = 64
STATE_SIZE = 128
KC = 4
FF = 2048
MICRO = 2
SPACE_CHANNELS = 1536
XBC = 1792


rope_base = 100000000000.0
norm_epsilon = 1e-05
masked_score = -1e30


def cut_along(x, dim, devices):
    lengths = x.shape
    blocks = x.reshape(*lengths[:dim], devices, lengths[dim] // devices, *lengths[dim + 1 :])
    return jnp.moveaxis(blocks, dim, 0)


def sum_at_owner(x, axis, dim):
    blocks = cut_along(x, dim, lax.axis_size(axis))
    arrived = lax.all_to_all(blocks, axis, split_axis=0, concat_axis=0, tiled=True)
    return arrived.astype(jnp.float32).sum(axis=0)


def joined_along(blocks, dim):
    lengths = list(blocks.shape[1:])
    lengths[dim] *= blocks.shape[0]
    return jnp.moveaxis(blocks, 0, dim).reshape(lengths)


def copy_for_each(x, axis):
    copies = jnp.broadcast_to(x, (lax.axis_size(axis), *x.shape))
    return lax.all_to_all(copies, axis, split_axis=0, concat_axis=0, tiled=True)


def collect(x, axis, dim):
    return joined_along(copy_for_each(x, axis), dim)


def from_behind(block, axis, distance):
    devices = range(lax.axis_size(axis))
    route = [(i - distance, i) for i in devices if i - distance in devices]
    return lax.ppermute(block, axis, route)


def entering(x, axis, join, neutral):
    place = lax.axis_index(axis)
    gathered = jax.tree.map(
        lambda a, kind: lax.all_gather(a.astype(kind), axis), x, (jnp.bfloat16, jnp.bfloat16)
    )
    state = jax.tree.map(lambda a, e: jnp.zeros_like(a) + jnp.asarray(e, a.dtype), x, neutral)

    def one(lap, state):
        return join(
            state,
            jax.tree.map(
                lambda a, own: lax.dynamic_index_in_dim(a, lap, 0, False).astype(own.dtype),
                gathered,
                x,
            ),
        )

    return lax.fori_loop(0, place, one, state)


def carried_in(x, axis, combine, identity):
    devices, index = (lax.axis_size(axis), lax.axis_index(axis))
    everything = jax.tree.map(
        lambda part, kind: lax.all_gather(part.astype(kind), axis),
        x,
        jax.tree.map(lambda a: jnp.bfloat16 if a.dtype == jnp.float32 else a.dtype, x),
    )
    start = jax.tree.map(
        lambda part, zero: jnp.broadcast_to(jnp.asarray(zero, part.dtype), part.shape), x, identity
    )

    def lap(k, before):
        at = devices - 1 - k
        reached = at > index
        new = combine(
            before, jax.tree.map(lambda part, own: part[at].astype(own.dtype), everything, x)
        )
        return jax.tree.map(lambda a, b: jnp.where(reached, a, b), new, before)

    return lax.fori_loop(0, devices, lap, start)


def in_one_piece(arrays, axis, dim, along):
    widths = [a.shape[along] for a in arrays]
    both = jnp.concatenate(arrays, axis=along)
    out = lax.all_gather(both, axis, axis=dim, tiled=True)
    return tuple(jnp.split(out, [sum(widths[:k]) for k in range(1, len(widths))], axis=along))


def sent_together(arrays, axis, dim, along):
    ends, at = ([], 0)
    for a in arrays[:-1]:
        at += a.shape[along]
        ends.append(at)
    both = jnp.concatenate(arrays, axis=along)
    return tuple(
        jnp.split(lax.psum_scatter(both, axis, scatter_dimension=dim, tiled=True), ends, axis=along)
    )


def norm_rows(value_rows, gain):
    return (
        value_rows
        * lax.rsqrt(jnp.mean(value_rows * value_rows, axis=-1, keepdims=True) + norm_epsilon)
        * gain
    )


def bf_dot(left, right):
    return jnp.dot(left, right, preferred_element_type=jnp.float32)


def grad_dot(left, right):
    return lax.dot_general(
        left, right, (((0,), (0,)), ((), ())), preferred_element_type=jnp.float32
    )


def back_dot(left, right):
    return lax.dot_general(
        left, right, (((1,), (1,)), ((), ())), preferred_element_type=jnp.float32
    )


def rotary_angles(value_rows, token_positions):
    half_width = value_rows.shape[-1] // 2
    frequency = rope_base ** (-jnp.arange(half_width, dtype=jnp.float32) / half_width)
    angles = token_positions.astype(jnp.float32)[:, None] * frequency[None, :]
    cosine = jnp.cos(angles)[:, None, :]
    sine_part = jnp.sin(angles)[:, None, :]
    first_half = value_rows[..., :half_width]
    second_half = value_rows[..., half_width:]
    return jnp.concatenate(
        [
            first_half * cosine - second_half * sine_part,
            second_half * cosine + first_half * sine_part,
        ],
        axis=-1,
    )


def pack_layout(lengths_row, count_of_blocks, rows_per_block):
    used_blocks = (lengths_row + rows_per_block - 1) // rows_per_block
    first_block = jnp.cumsum(used_blocks) - used_blocks
    block_order = jnp.arange(count_of_blocks, dtype=jnp.int32)
    covers = (
        (block_order[:, None] >= first_block[None, :])
        & (block_order[:, None] < (first_block + used_blocks)[None, :])
    ).astype(jnp.int32)
    occupied = jnp.sum(covers, axis=1) > 0
    slot_order = jnp.arange(lengths_row.shape[0], dtype=jnp.int32)
    segment = jnp.where(occupied, jnp.sum(covers * slot_order[None, :], axis=1), -1)
    begins = jnp.sum(covers * first_block[None, :], axis=1)
    seq_length = jnp.sum(covers * lengths_row[None, :], axis=1)
    within = (block_order - begins)[:, None] * rows_per_block + jnp.arange(
        rows_per_block, dtype=jnp.int32
    )[None, :]
    is_valid = occupied[:, None] & (within < seq_length[:, None])
    carry_flag = occupied & (block_order > begins)
    return (segment, within, is_valid, carry_flag)


def allowed_mask(segment, is_valid, query_start, rows_of_queries):
    rows_per_block = is_valid.shape[1]
    token_segment = jnp.repeat(segment, rows_per_block)
    token_valid = is_valid.reshape(-1)
    key_order = jnp.arange(token_valid.shape[0], dtype=jnp.int32)
    query_order = query_start + jnp.arange(rows_of_queries, dtype=jnp.int32)
    query_segment = lax.dynamic_slice_in_dim(token_segment, query_start, rows_of_queries, 0)
    same_sequence = (
        (query_segment[:, None] == token_segment[None, :])
        & (key_order[None, :] <= query_order[:, None])
        & token_valid[None, :]
    )
    return same_sequence | (key_order[None, :] == query_order[:, None])


def conv_apply(extended, kernel, offset):
    out_rows = extended.shape[-2] - kernel.shape[0] + 1
    total_sum = offset
    for tap in range(kernel.shape[0]):
        total_sum = total_sum + kernel[tap] * extended[..., tap : tap + out_rows, :]
    return jax.nn.silu(total_sum)


def block_decay(step, decay_log):
    return jnp.cumsum(step * (-jnp.exp(decay_log))[None, :], axis=0)


def block_output(state_inputs, input_b, output_c, step, decay_log, skip_gain, incoming):
    cumul = block_decay(step, decay_log)
    count_of_rows = state_inputs.shape[0]
    causal = (jnp.arange(count_of_rows)[:, None] >= jnp.arange(count_of_rows)[None, :])[:, :, None]
    gaps = cumul[:, None, :] - cumul[None, :, :]
    decay = jnp.where(causal, jnp.exp(jnp.where(causal, gaps, 0.0)), 0.0)
    intersection = jnp.dot(output_c, input_b.T, precision=lax.Precision.HIGHEST)
    mixing = intersection[:, :, None] * decay * step[None, :, :]
    inner = jnp.einsum("tsh,shp->thp", mixing, state_inputs, precision=lax.Precision.HIGHEST)
    carried = (
        jnp.einsum("tn,hpn->thp", output_c, incoming, precision=lax.Precision.HIGHEST)
        * jnp.exp(cumul)[:, :, None]
    )
    return inner + carried + skip_gain[None, :, None] * state_inputs


def block_state(state_inputs, input_b, step, decay_log):
    cumul = block_decay(step, decay_log)
    tail = jnp.exp(cumul[-1][None, :] - cumul) * step
    local_state = jnp.einsum(
        "sh,shp,sn->hpn", tail, state_inputs, input_b, precision=lax.Precision.HIGHEST
    )
    return (local_state, jnp.exp(cumul[-1]))


def link_states(earlier, later):
    return (later[0] * earlier[0], later[0][:, None, None] * earlier[1] + later[1])


def pick_item(stacked_tree, position):
    return jax.tree.map(
        lambda stacked: lax.dynamic_index_in_dim(stacked, position, 0, keepdims=False), stacked_tree
    )


def unpack_weights(weights):
    (
        gains,
        mix_weight,
        step_weight,
        conv_weight,
        conv_offset,
        out_weight,
        gate_up_weight,
        down_weight,
    ) = weights
    return (
        gains.astype(jnp.float32),
        mix_weight,
        step_weight,
        conv_weight.astype(jnp.float32),
        conv_offset.astype(jnp.float32),
        out_weight,
        gate_up_weight,
        down_weight,
    )


def local_layout(layout, rank_pos):
    segment, within, is_valid, carry_all = layout
    token_positions = lax.dynamic_index_in_dim(within, rank_pos, 0, keepdims=False)
    row_valid = lax.dynamic_index_in_dim(is_valid, rank_pos, 0, keepdims=False).astype(jnp.float32)[
        :, None
    ]
    carry_flag = lax.dynamic_index_in_dim(carry_all, rank_pos, 0, keepdims=False).astype(
        jnp.float32
    )
    allowed = allowed_mask(
        segment, is_valid, rank_pos * token_positions.shape[0], token_positions.shape[0]
    )
    return (token_positions, row_valid, carry_flag, allowed)


def ssm_inputs(extended, conv_weight, conv_offset, step_raw, heads):
    activated_rows = conv_apply(extended, conv_weight, conv_offset)
    count_of_rows = activated_rows.shape[0]
    state_inputs = activated_rows[:, :SPACE_CHANNELS].reshape(
        count_of_rows, MIXER_HEADS, MIXER_HEAD_SIZE
    )
    step = jax.nn.softplus(step_raw + heads[0])
    return (
        state_inputs,
        activated_rows[:, SPACE_CHANNELS : SPACE_CHANNELS + STATE_SIZE],
        activated_rows[:, SPACE_CHANNELS + STATE_SIZE :],
        step,
    )


def split_kv(packed_key_value):
    packed_key_rows = packed_key_value[:, : KEY_VALUE_HEADS * HEAD_SIZE].reshape(
        packed_key_value.shape[0], KEY_VALUE_HEADS, HEAD_SIZE
    )
    packed_value_rows = packed_key_value[:, KEY_VALUE_HEADS * HEAD_SIZE :].reshape(
        packed_key_value.shape[0], KEY_VALUE_HEADS, HEAD_SIZE
    )
    return (packed_key_rows, packed_value_rows)


def attend_forward(query_vectors, packed_key_value, allowed):
    rows_of_queries = query_vectors.shape[0]
    grouped_heads = query_vectors.reshape(
        rows_of_queries, KEY_VALUE_HEADS, QUERY_HEADS // KEY_VALUE_HEADS, HEAD_SIZE
    )
    packed_key_rows, packed_value_rows = split_kv(packed_key_value)
    raw_scores = jnp.einsum(
        "qgrd,kgd->grqk", grouped_heads, packed_key_rows, preferred_element_type=jnp.float32
    )
    scores = jnp.where(allowed[None, None], raw_scores * HEAD_SIZE ** (-0.5), masked_score)
    peak = jnp.max(scores, axis=-1, keepdims=True)
    expo_scores = jnp.exp(scores - peak)
    total_sum = jnp.sum(expo_scores, axis=-1, keepdims=True)
    probs = expo_scores / total_sum
    log_total = peak + jnp.log(total_sum)
    attended = jnp.einsum(
        "grqk,kgd->qgrd",
        probs.astype(jnp.bfloat16),
        packed_value_rows,
        preferred_element_type=jnp.float32,
    )
    return (attended.reshape(rows_of_queries, QUERY_HEADS * HEAD_SIZE), log_total)


def attend_backward(query_vectors, packed_key_value, allowed, log_total, gradient_attended):
    rows_of_queries = query_vectors.shape[0]
    grouped_heads = query_vectors.reshape(
        rows_of_queries, KEY_VALUE_HEADS, QUERY_HEADS // KEY_VALUE_HEADS, HEAD_SIZE
    )
    gradient_grouped = gradient_attended.reshape(
        rows_of_queries, KEY_VALUE_HEADS, QUERY_HEADS // KEY_VALUE_HEADS, HEAD_SIZE
    )
    packed_key_rows, packed_value_rows = split_kv(packed_key_value)
    raw_scores = jnp.einsum(
        "qgrd,kgd->grqk", grouped_heads, packed_key_rows, preferred_element_type=jnp.float32
    )
    scores = jnp.where(allowed[None, None], raw_scores * HEAD_SIZE ** (-0.5), masked_score)
    probs = jnp.exp(scores - log_total)
    grad_probs = jnp.einsum(
        "qgrd,kgd->grqk", gradient_grouped, packed_value_rows, preferred_element_type=jnp.float32
    )
    grad_scores = probs * (grad_probs - jnp.sum(probs * grad_probs, axis=-1, keepdims=True))
    grad_raw = (jnp.where(allowed[None, None], grad_scores, 0.0) * HEAD_SIZE ** (-0.5)).astype(
        jnp.bfloat16
    )
    probs_low = probs.astype(jnp.bfloat16)
    grad_queries = jnp.einsum(
        "grqk,kgd->qgrd", grad_raw, packed_key_rows, preferred_element_type=jnp.float32
    ).reshape(rows_of_queries, QUERY_HEADS * HEAD_SIZE)
    grad_keys = jnp.einsum(
        "grqk,qgrd->kgd", grad_raw, grouped_heads, preferred_element_type=jnp.float32
    ).reshape(rows_of_queries * lax.axis_size("fsdp"), KEY_VALUE_HEADS * HEAD_SIZE)
    grad_values = jnp.einsum(
        "grqk,qgrd->kgd", probs_low, gradient_grouped, preferred_element_type=jnp.float32
    ).reshape(rows_of_queries * lax.axis_size("fsdp"), KEY_VALUE_HEADS * HEAD_SIZE)
    gradient_own_key_value = sum_at_owner(
        jnp.concatenate([grad_keys, grad_values], axis=1).astype(jnp.bfloat16), "fsdp", 0
    )
    return (grad_queries, gradient_own_key_value)


def layer_forward(weights, heads, layer_in, layout, rank_pos):
    (
        gains,
        mix_weight,
        step_weight,
        conv_weight,
        conv_offset,
        out_weight,
        gate_up_weight,
        down_weight,
    ) = unpack_weights(weights)
    token_positions, row_valid, carry_flag, allowed = local_layout(layout, rank_pos)
    count_of_rows = layer_in.shape[0]
    attention_offset = SPACE_CHANNELS + XBC
    normed = norm_rows(layer_in, gains[0]).astype(jnp.bfloat16)
    mixed_rows = bf_dot(normed, mix_weight)
    step_raw = bf_dot(normed, step_weight)
    conv_in = mixed_rows[:, SPACE_CHANNELS : SPACE_CHANNELS + XBC].astype(jnp.bfloat16)
    query_vectors = rotary_angles(
        mixed_rows[:, attention_offset : attention_offset + QUERY_HEADS * HEAD_SIZE].reshape(
            count_of_rows, QUERY_HEADS, HEAD_SIZE
        ),
        token_positions,
    ).astype(jnp.bfloat16)
    local_key_rows = rotary_angles(
        mixed_rows[
            :,
            attention_offset
            + QUERY_HEADS * HEAD_SIZE : attention_offset
            + (QUERY_HEADS + KEY_VALUE_HEADS) * HEAD_SIZE,
        ].reshape(count_of_rows, KEY_VALUE_HEADS, HEAD_SIZE),
        token_positions,
    )
    own_kv = jnp.concatenate(
        [
            local_key_rows.reshape(count_of_rows, KEY_VALUE_HEADS * HEAD_SIZE),
            mixed_rows[:, attention_offset + (QUERY_HEADS + KEY_VALUE_HEADS) * HEAD_SIZE :],
        ],
        axis=1,
    ).astype(jnp.bfloat16)
    packed_key_value = collect(own_kv, "fsdp", 0)
    attended, log_total = attend_forward(query_vectors, packed_key_value, allowed)
    edge_rows = from_behind(conv_in[count_of_rows - (KC - 1) :], "fsdp", 1)
    extended = jnp.concatenate(
        [edge_rows.astype(jnp.float32) * carry_flag, conv_in.astype(jnp.float32)], axis=0
    )
    state_inputs, input_b, output_c, step = ssm_inputs(
        extended, conv_weight, conv_offset, step_raw, heads
    )
    local_state, decay_total = block_state(state_inputs, input_b, step, heads[1])
    decay_kept = decay_total * carry_flag
    prior = entering(
        (decay_kept, local_state),
        "fsdp",
        link_states,
        (jnp.ones_like(decay_kept), jnp.zeros_like(local_state)),
    )
    incoming = prior[1] * carry_flag
    ssm_out = block_output(
        state_inputs, input_b, output_c, step, heads[1], heads[2], incoming
    ).reshape(count_of_rows, SPACE_CHANNELS)
    gated = ssm_out * jax.nn.silu(mixed_rows[:, :SPACE_CHANNELS])
    joined = jnp.concatenate([attended, gated], axis=1).astype(jnp.bfloat16)
    resid = layer_in + bf_dot(joined, out_weight)
    normed_two = norm_rows(resid, gains[1]).astype(jnp.bfloat16)
    gate_up = bf_dot(normed_two, gate_up_weight)
    hidden = (jax.nn.silu(gate_up[:, :FF]) * gate_up[:, FF:]).astype(jnp.bfloat16)
    result = row_valid * (resid + bf_dot(hidden, down_weight))
    kept = (
        layer_in,
        normed,
        mixed_rows,
        step_raw,
        extended,
        query_vectors,
        packed_key_value,
        log_total,
        decay_kept,
        incoming,
        ssm_out,
        joined,
        resid,
        normed_two,
        gate_up,
        hidden,
    )
    return (result, kept)


def swiglu(gate_up):
    return jax.nn.silu(gate_up[:, :FF]) * gate_up[:, FF:]


def gate_product(ssm_values, gate_values):
    return ssm_values * jax.nn.silu(gate_values)


def step_function(raw_values, bias_values):
    return jax.nn.softplus(raw_values + bias_values)


def layer_backward(weights, heads, kept, arriving, layout, rank_pos):
    (
        gains,
        mix_weight,
        step_weight,
        conv_weight,
        conv_offset,
        out_weight,
        gate_up_weight,
        down_weight,
    ) = unpack_weights(weights)
    (
        layer_in,
        normed,
        mixed_rows,
        step_raw,
        extended,
        query_vectors,
        packed_key_value,
        log_total,
        decay_kept,
        incoming,
        ssm_out,
        joined,
        resid,
        normed_two,
        gate_up,
        hidden,
    ) = kept
    token_positions, row_valid, carry_flag, allowed = local_layout(layout, rank_pos)
    count_of_rows = layer_in.shape[0]
    attention_offset = SPACE_CHANNELS + XBC
    grad_resid = arriving * row_valid
    grad_ffn = grad_resid.astype(jnp.bfloat16)
    grad_hidden = back_dot(grad_ffn, down_weight)
    _, swiglu_pull = jax.vjp(swiglu, gate_up)
    grad_gate_up = swiglu_pull(grad_hidden)[0].astype(jnp.bfloat16)
    grad_normed_two = back_dot(grad_gate_up, gate_up_weight)
    _, second_pull = jax.vjp(norm_rows, resid, gains[1])
    grad_resid_norm, grad_gain_two = second_pull(grad_normed_two)
    grad_resid = grad_resid + grad_resid_norm
    grad_branch = grad_resid.astype(jnp.bfloat16)
    grad_joined = back_dot(grad_branch, out_weight)
    gradient_attended = grad_joined[:, : QUERY_HEADS * HEAD_SIZE].astype(jnp.bfloat16)
    _, gate_pull = jax.vjp(gate_product, ssm_out, mixed_rows[:, :SPACE_CHANNELS])
    gradient_mixer_state, grad_gate_z = gate_pull(grad_joined[:, QUERY_HEADS * HEAD_SIZE :])
    state_inputs, input_b, output_c, step = ssm_inputs(
        extended, conv_weight, conv_offset, step_raw, heads
    )
    _, output_derivative = jax.vjp(
        block_output, state_inputs, input_b, output_c, step, heads[1], heads[2], incoming
    )
    grad_x_one, grad_b_one, grad_c, grad_step_one, grad_decay_one, grad_skip, grad_incoming = (
        output_derivative(gradient_mixer_state.reshape(count_of_rows, MIXER_HEADS, MIXER_HEAD_SIZE))
    )
    after = carried_in(
        (decay_kept, grad_incoming * carry_flag),
        "fsdp",
        link_states,
        (jnp.ones_like(decay_kept), jnp.zeros_like(grad_incoming)),
    )
    grad_state = after[1]
    grad_total = jnp.sum(grad_state * incoming, axis=(1, 2))
    _, state_pull = jax.vjp(block_state, state_inputs, input_b, step, heads[1])
    grad_x_two, grad_b_two, grad_step_two, grad_decay_two = state_pull((grad_state, grad_total))
    grad_activated = jnp.concatenate(
        [
            (grad_x_one + grad_x_two).reshape(count_of_rows, SPACE_CHANNELS),
            grad_b_one + grad_b_two,
            grad_c,
        ],
        axis=1,
    )
    _, conv_pull = jax.vjp(conv_apply, extended, conv_weight, conv_offset)
    grad_extended, grad_kernel, grad_offset = conv_pull(grad_activated)
    back_edge = from_behind(grad_extended[: KC - 1] * carry_flag, "fsdp", -1)
    grad_conv_in = grad_extended[KC - 1 :] + jnp.concatenate(
        [jnp.zeros((count_of_rows - (KC - 1), XBC), jnp.float32), back_edge], axis=0
    )
    _, step_pull = jax.vjp(step_function, step_raw, heads[0])
    grad_step_raw, grad_bias = step_pull(grad_step_one + grad_step_two)
    grad_step_low = grad_step_raw.astype(jnp.bfloat16)
    grad_queries, gradient_own_key_value = attend_backward(
        query_vectors, packed_key_value, allowed, log_total, gradient_attended
    )
    query_raw = mixed_rows[
        :, attention_offset : attention_offset + QUERY_HEADS * HEAD_SIZE
    ].reshape(count_of_rows, QUERY_HEADS, HEAD_SIZE)
    key_unrotated = mixed_rows[
        :,
        attention_offset
        + QUERY_HEADS * HEAD_SIZE : attention_offset
        + (QUERY_HEADS + KEY_VALUE_HEADS) * HEAD_SIZE,
    ].reshape(count_of_rows, KEY_VALUE_HEADS, HEAD_SIZE)
    _, query_pull = jax.vjp(
        lambda raw_values: rotary_angles(raw_values, token_positions), query_raw
    )
    grad_query_raw = query_pull(grad_queries.reshape(count_of_rows, QUERY_HEADS, HEAD_SIZE))[0]
    _, key_derivative = jax.vjp(
        lambda raw_values: rotary_angles(raw_values, token_positions), key_unrotated
    )
    gradient_key_unrotated = key_derivative(
        gradient_own_key_value[:, : KEY_VALUE_HEADS * HEAD_SIZE].reshape(
            count_of_rows, KEY_VALUE_HEADS, HEAD_SIZE
        )
    )[0]
    grad_mixed = jnp.concatenate(
        [
            grad_gate_z,
            grad_conv_in,
            grad_query_raw.reshape(count_of_rows, QUERY_HEADS * HEAD_SIZE),
            gradient_key_unrotated.reshape(count_of_rows, KEY_VALUE_HEADS * HEAD_SIZE),
            gradient_own_key_value[:, KEY_VALUE_HEADS * HEAD_SIZE :],
        ],
        axis=1,
    ).astype(jnp.bfloat16)
    grad_normed = back_dot(grad_mixed, mix_weight) + back_dot(grad_step_low, step_weight)
    _, first_pull = jax.vjp(norm_rows, layer_in, gains[0])
    grad_in_norm, grad_gain_one = first_pull(grad_normed)
    grad_input = grad_resid + grad_in_norm
    heads_grad = jnp.stack([grad_bias, grad_decay_one + grad_decay_two, grad_skip])
    small_grads = (jnp.stack([grad_gain_one, grad_gain_two]), grad_kernel, grad_offset, heads_grad)
    row_terms = (
        normed,
        grad_mixed,
        grad_step_low,
        joined,
        grad_branch,
        normed_two,
        grad_gate_up,
        hidden,
        grad_ffn,
    )
    return (grad_input, small_grads, row_terms)


def local(
    layer_input,
    cotangent,
    seq_lengths,
    norm_gains,
    w_mix,
    w_step,
    conv_kernel,
    conv_bias,
    head_params,
    w_out,
    w_gate_up,
    w_down,
):
    sections = lax.axis_size("section")
    section_pos = lax.axis_index("section")
    ranks = lax.axis_size("fsdp")
    rank_pos = lax.axis_index("fsdp")
    count_of_rows = layer_input.shape[2]
    model_width = layer_input.shape[3]
    turn_count = MICRO + sections - 1
    forward_weights = (
        lax.all_gather(norm_gains[0], "fsdp", axis=1, tiled=True),
        *in_one_piece((w_mix[0], w_step[0]), "fsdp", 0, 1),
        lax.all_gather(conv_kernel[0], "fsdp", axis=1, tiled=True),
        lax.all_gather(conv_bias[0], "fsdp", axis=0, tiled=True),
        lax.all_gather(w_out[0], "fsdp", axis=0, tiled=True),
        lax.all_gather(w_gate_up[0], "fsdp", axis=0, tiled=True),
        lax.all_gather(w_down[0], "fsdp", axis=0, tiled=True),
    )
    heads = head_params[0]
    layouts = jax.vmap(lambda lengths_row: pack_layout(lengths_row, ranks, count_of_rows))(
        seq_lengths[:, 0]
    )
    own_inputs = layer_input[:, 0].astype(jnp.float32)
    top_grads = cotangent[:, 0].astype(jnp.float32)
    micro_order = jnp.arange(MICRO, dtype=jnp.int32)
    activations = jnp.zeros((MICRO, count_of_rows, model_width), jnp.bfloat16)
    received = jnp.zeros((count_of_rows, model_width), jnp.bfloat16)
    kept_list = []
    for forward_turn in range(turn_count):
        micro_index = forward_turn - section_pos
        active = (micro_index >= 0) & (micro_index < MICRO)
        picked = jnp.clip(micro_index, 0, MICRO - 1)
        layout = pick_item(layouts, picked)
        own_input = lax.dynamic_index_in_dim(own_inputs, picked, 0, keepdims=False)
        layer_in = jnp.where(section_pos == 0, own_input, received.astype(jnp.float32))
        result, kept = layer_forward(forward_weights, heads, layer_in, layout, rank_pos)
        result_low = result.astype(jnp.bfloat16)
        chosen = ((micro_order == micro_index) & active)[:, None, None]
        activations = jnp.where(chosen, result_low[None], activations)
        kept_list.append(kept)
        if forward_turn + 1 < turn_count:
            received = from_behind(result_low, "section", 1)
    stacked_kept = jax.tree.map(lambda *items: jnp.stack(items), *kept_list)
    backward_weights = (
        lax.all_gather(norm_gains[0], "fsdp", axis=1, tiled=True),
        *in_one_piece((w_mix[0], w_step[0]), "fsdp", 0, 1),
        lax.all_gather(conv_kernel[0], "fsdp", axis=1, tiled=True),
        lax.all_gather(conv_bias[0], "fsdp", axis=0, tiled=True),
        lax.all_gather(w_out[0], "fsdp", axis=0, tiled=True),
        lax.all_gather(w_gate_up[0], "fsdp", axis=0, tiled=True),
        lax.all_gather(w_down[0], "fsdp", axis=0, tiled=True),
    )
    input_grads = jnp.zeros((MICRO, count_of_rows, model_width), jnp.float32)
    back_received = jnp.zeros((count_of_rows, model_width), jnp.bfloat16)
    small_total = ()
    weight_rows = []
    for back_turn in range(turn_count):
        micro_index = back_turn - (sections - 1 - section_pos)
        active = (micro_index >= 0) & (micro_index < MICRO)
        picked = jnp.clip(micro_index, 0, MICRO - 1)
        source = jnp.clip(micro_index + section_pos, 0, turn_count - 1)
        kept = pick_item(stacked_kept, source)
        layout = pick_item(layouts, picked)
        top_grad = lax.dynamic_index_in_dim(top_grads, picked, 0, keepdims=False)
        arriving = jnp.where(
            section_pos == sections - 1, top_grad, back_received.astype(jnp.float32)
        ) * active.astype(jnp.float32)
        grad_input, small_grads, row_terms = layer_backward(
            backward_weights, heads, kept, arriving, layout, rank_pos
        )
        chosen = ((micro_order == micro_index) & active)[:, None, None]
        input_grads = jnp.where(chosen, grad_input[None], input_grads)
        if back_turn == 0:
            small_total = small_grads
        else:
            small_total = jax.tree.map(jnp.add, small_total, small_grads)
        weight_rows.append(row_terms)
        if back_turn + 1 < turn_count:
            back_received = from_behind(grad_input.astype(jnp.bfloat16), "section", -1)
    row_stack = [jnp.concatenate(items, axis=0) for items in zip(*weight_rows)]
    (
        normed_rows,
        grad_mix_rows,
        grad_step_rows,
        joined_rows,
        grad_branch_rows,
        normed_two_rows,
        grad_gate_up_rows,
        hidden_rows,
        grad_ffn_rows,
    ) = row_stack
    grad_mix = grad_dot(normed_rows, grad_mix_rows)
    grad_step = grad_dot(normed_rows, grad_step_rows)
    grad_out_weight = grad_dot(joined_rows, grad_branch_rows)
    grad_gate_up_weight = grad_dot(normed_two_rows, grad_gate_up_rows)
    grad_down_weight = grad_dot(hidden_rows, grad_ffn_rows)
    gain_grads, kernel_grads, offset_grads, heads_grads = small_total
    tiled = jnp.broadcast_to(heads_grads[None], (ranks,) + heads_grads.shape)
    (
        gain_part,
        mix_part,
        step_part,
        kernel_part,
        offset_part,
        out_part,
        gate_up_part,
        down_part,
        heads_part,
    ) = (
        lax.psum_scatter(
            gain_grads.astype(jnp.bfloat16), "fsdp", scatter_dimension=1, tiled=True
        ).astype(jnp.float32),
        *tuple(
            (
                part.astype(jnp.float32)
                for part in sent_together(
                    (grad_mix.astype(jnp.bfloat16), grad_step.astype(jnp.bfloat16)), "fsdp", 0, 1
                )
            )
        ),
        lax.psum_scatter(
            kernel_grads.astype(jnp.bfloat16), "fsdp", scatter_dimension=1, tiled=True
        ).astype(jnp.float32),
        lax.psum_scatter(
            offset_grads.astype(jnp.bfloat16), "fsdp", scatter_dimension=0, tiled=True
        ).astype(jnp.float32),
        lax.psum_scatter(
            grad_out_weight.astype(jnp.bfloat16), "fsdp", scatter_dimension=0, tiled=True
        ).astype(jnp.float32),
        lax.psum_scatter(
            grad_gate_up_weight.astype(jnp.bfloat16), "fsdp", scatter_dimension=0, tiled=True
        ).astype(jnp.float32),
        lax.psum_scatter(
            grad_down_weight.astype(jnp.bfloat16), "fsdp", scatter_dimension=0, tiled=True
        ).astype(jnp.float32),
        lax.psum_scatter(
            tiled.astype(jnp.bfloat16), "fsdp", scatter_dimension=0, tiled=True
        ).astype(jnp.float32),
    )
    (
        gain_sum,
        mix_sum,
        step_sum,
        kernel_sum,
        offset_sum,
        out_sum,
        gate_up_sum,
        down_sum,
        heads_sum,
    ) = (
        lax.psum(gain_part.astype(jnp.bfloat16), "rep").astype(jnp.float32),
        lax.psum(mix_part.astype(jnp.bfloat16), "rep").astype(jnp.float32),
        lax.psum(step_part.astype(jnp.bfloat16), "rep").astype(jnp.float32),
        lax.psum(kernel_part.astype(jnp.bfloat16), "rep").astype(jnp.float32),
        lax.psum(offset_part.astype(jnp.bfloat16), "rep").astype(jnp.float32),
        lax.psum(out_part.astype(jnp.bfloat16), "rep").astype(jnp.float32),
        lax.psum(gate_up_part.astype(jnp.bfloat16), "rep").astype(jnp.float32),
        lax.psum(down_part.astype(jnp.bfloat16), "rep").astype(jnp.float32),
        lax.psum(heads_part.astype(jnp.bfloat16), "rep").astype(jnp.float32),
    )
    return (
        activations[None, :, None],
        input_grads[None, :, None],
        gain_sum[None],
        mix_sum[None],
        step_sum[None],
        kernel_sum[None],
        offset_sum[None],
        heads_sum,
        out_sum[None],
        gate_up_sum[None],
        down_sum[None],
    )


def solution(mesh):
    in_specs = (
        P(None, "rep", "fsdp", None),
        P(None, "rep", "fsdp", None),
        P(None, "rep", None),
        P("section", None, "fsdp"),
        P("section", "fsdp", None),
        P("section", "fsdp", None),
        P("section", None, "fsdp"),
        P("section", "fsdp"),
        P("section", None, None),
        P("section", "fsdp", None),
        P("section", "fsdp", None),
        P("section", "fsdp", None),
    )
    out_specs = (
        P("section", None, "rep", "fsdp", None),
        P("section", None, "rep", "fsdp", None),
        P("section", None, "fsdp"),
        P("section", "fsdp", None),
        P("section", "fsdp", None),
        P("section", None, "fsdp"),
        P("section", "fsdp"),
        P("section", None, None),
        P("section", "fsdp", None),
        P("section", "fsdp", None),
        P("section", "fsdp", None),
    )
    return jax.shard_map(local, mesh=mesh, in_specs=in_specs, out_specs=out_specs, check_vma=False)
```

profile of v0, /device:TPU:1, one launch (start us, length us, event | category | flops | bytes accessed | tf_op | source)
XLA Modules:
  0.0 1957.9 jit_solution(15542281274582671878)
XLA Ops:
  16.0 29.1 %all-gather = bf16[1,2,1024]{1,0,2:T(2,128)(2,1)S(1)} all-gather(bf16[1,2,64]{1,0,2:T(2,128)(2,1)S(1)} %copy.1020), channel_id=2, replica_groups=mesh['section'=2,'fsdp'=16,'rep'=4] {'fsdp'}, dimensions={2}, use_global_device_ids=true | all-gather | bytes 4352 | tf_op jit(solution)/shard_map/all_gather | solution.py:624
  47.2 33.3 %all-reduce.51 = bf16[1792]{0:T(1024)(128)(2,1)S(1)} all-reduce(bf16[1792]{0:T(1024)(128)(2,1)S(1)} %dynamic-update-slice), channel_id=3, replica_groups=mesh['section'=2,'fsdp'=16,'rep'=4] {'fsdp'}, use_global_device_ids=true, to_apply=%add.51 | all-reduce | flops 1792 | bytes 7168
  80.6 23.9 %all-gather.2 = bf16[1,4,1792]{1,0,2:T(2,128)(2,1)S(1)} all-gather(bf16[1,4,112]{1,0,2:T(2,128)(2,1)S(1)} %copy.1027), channel_id=4, replica_groups=mesh['section'=2,'fsdp'=16,'rep'=4] {'fsdp'}, dimensions={2}, use_global_device_ids=true | all-gather | bytes 15232 | tf_op jit(solution)/shard_map/all_gather | solution.py:626
  112.4 37.4 %slice_reduce_fusion.3 = (f32[1792]{0:T(1024)S(1)}, f32[1792]{0:T(1024)S(1)}, f32[1792]{0:T(1024)S(1)}, f32[1792]{0:T(1024)S(1)}) fusion(f32[1,4,1792]{1,0,2:T(1,128)S(1)} %convert_element_type.807), kind=kLoop, calls=%fused_computation.259 | loop fusion | bytes 57344 | tf_op jit(solution)/shard_map/slice | solution.py:198
  174.5 6.5 all-to-all-start
  181.2 27.0 %all-gather.12 = bf16[16,1,24]{2,1,0:T(2,128)(2,1)S(1)} all-gather(bf16[1,1,24]{2,1,0:T(2,128)(2,1)S(1)} %fusion.760), channel_id=1, replica_groups=mesh['section'=2,'fsdp'=16,'rep'=4] {'fsdp'}, dimensions={0}, use_global_device_ids=true | all-gather | bytes 816 | tf_op jit(solution)/shard_map/all_gather | solution.py:60
  212.0 22.0 %all-gather.31.cloned.1.call-done = bf16[384,64,128]{2,1,0:T(8,128)(2,1)} async-done(((bf16[24,64,128]{2,1,0:T(8,128)(2,1)}), bf16[384,64,128]{2,1,0:T(8,128)(2,1)}) %all-gather.31.cloned.1.call-update) | async-done | bytes 6291472 | tf_op jit(solution)/shard_map/all_gather | solution.py:60
  240.1 50.8 %all-gather.33.cloned.1.call-done = bf16[1,2048,1024]{2,1,0:T(8,128)(2,1)} async-done(((bf16[1,128,1024]{2,1,0:T(8,128)(2,1)}), bf16[1,2048,1024]{2,1,0:T(8,128)(2,1)}) %all-gather.33.cloned.1.call-update) | async-done | bytes 4194320 | tf_op jit(solution)/shard_map/all_gather | solution.py:628
  294.7 69.9 %all-gather.35.cloned.1.call-done = bf16[1,1024,4096]{2,1,0:T(8,128)(2,1)} async-done(((bf16[1,64,4096]{2,1,0:T(8,128)(2,1)}), bf16[1,1024,4096]{2,1,0:T(8,128)(2,1)}) %all-gather.35.cloned.1.call-update) | async-done | bytes 8388624 | tf_op jit(solution)/shard_map/all_gather | solution.py:629
  369.8 50.9 %all-gather.37.cloned.1.call-done = bf16[1,2048,1024]{2,1,0:T(8,128)(2,1)} async-done(((bf16[1,128,1024]{2,1,0:T(8,128)(2,1)}), bf16[1,2048,1024]{2,1,0:T(8,128)(2,1)}) %all-gather.37.cloned.1.call-update) | async-done | bytes 4194320 | tf_op jit(solution)/shard_map/all_gather | solution.py:630
  453.1 8.2 all-to-all-start.1
  461.5 27.3 %all-gather.13 = bf16[16,1,24]{2,1,0:T(2,128)(2,1)S(1)} all-gather(bf16[1,1,24]{2,1,0:T(2,128)(2,1)S(1)} %fusion.759), channel_id=1, replica_groups=mesh['section'=2,'fsdp'=16,'rep'=4] {'fsdp'}, dimensions={0}, use_global_device_ids=true | all-gather | bytes 816 | tf_op jit(solution)/shard_map/all_gather | solution.py:60
  494.3 27.2 %all-gather.39.cloned.1.call-done = bf16[384,64,128]{2,1,0:T(8,128)(2,1)} async-done(((bf16[24,64,128]{2,1,0:T(8,128)(2,1)}), bf16[384,64,128]{2,1,0:T(8,128)(2,1)}) %all-gather.39.cloned.1.call-update) | async-done | bytes 6291472 | tf_op jit(solution)/shard_map/all_gather | solution.py:60
  573.8 21.6 %all-to-all-start.2 = ((bf16[16,64,256]{2,1,0:T(8,128)(2,1)}), bf16[16,64,256]{2,1,0:T(8,128)(2,1)S(1)}, u32[]{:S(2)}, u32[]{:S(2)}) async-start(bf16[16,64,256]{2,1,0:T(8,128)(2,1)} %broadcast_in_dim.591), calls=%async_computation.2 | async-start | bytes 1048576 | tf_op jit(solution)/shard_map/all_to_all | solution.py:44
  603.1 24.3 %all-gather.14 = bf16[16,1,24]{2,1,0:T(2,128)(2,1)S(1)} all-gather(bf16[1,1,24]{2,1,0:T(2,128)(2,1)S(1)} %fusion.758), channel_id=1, replica_groups=mesh['section'=2,'fsdp'=16,'rep'=4] {'fsdp'}, dimensions={0}, use_global_device_ids=true | all-gather | bytes 816 | tf_op jit(solution)/shard_map/all_gather | solution.py:60
  634.5 13.8 all-gather.41.cloned.1.call-done
  708.3 36.9 %all-gather.15 = bf16[16,1,24]{2,1,0:T(2,128)(2,1)S(1)} all-gather(bf16[1,1,24]{2,1,0:T(2,128)(2,1)S(1)} %get-tuple-element.1027), channel_id=1, replica_groups=mesh['section'=2,'fsdp'=16,'rep'=4] {'fsdp'}, dimensions={0}, use_global_device_ids=true | all-gather | bytes 816 | tf_op jit(solution)/shard_map/all_gather | solution.py:80
  838.6 38.2 %while.87 = (s32[]{:T(128)}, f32[24,64,128]{2,1,0:T(8,128)S(1)}, s32[]{:T(128)}, bf16[16,24]{1,0:T(8,128)(2,1)}, bf16[16,24,64,128]{3,2,1,0:T(8,128)(2,1)}, /*index=5*/s32[]{:T(128)}, s32[]{:T(128)}, s32[]{:T(128)}, s32[]{:T(128)}) while((s32[]{:T(128)}, f32[24,64,128]{2,1,0:T(8,128)S(1)}, s32[]{:T(128)}, ...), condition=%wide.region_30.31_spmd.clone, body=%wide.region_29.30_spmd.clone.sunk | while | flops 983072 | bytes 1966495 | solution.py:96
  967.2 24.6 %all-gather.16 = bf16[16,1,24]{2,1,0:T(2,128)(2,1)S(1)} all-gather(bf16[1,1,24]{2,1,0:T(2,128)(2,1)} %get-tuple-element.1026), channel_id=1, replica_groups=mesh['section'=2,'fsdp'=16,'rep'=4] {'fsdp'}, dimensions={0}, use_global_device_ids=true | all-gather | bytes 816 | tf_op jit(solution)/shard_map/all_gather | solution.py:80
  1077.9 38.5 %while.88 = (s32[]{:T(128)}, f32[24,64,128]{2,1,0:T(8,128)S(1)}, s32[]{:T(128)}, bf16[16,24]{1,0:T(8,128)(2,1)}, bf16[16,24,64,128]{3,2,1,0:T(8,128)(2,1)}, /*index=5*/s32[]{:T(128)}, s32[]{:T(128)}, s32[]{:T(128)}, s32[]{:T(128)}) while((s32[]{:T(128)}, f32[24,64,128]{2,1,0:T(8,128)S(1)}, s32[]{:T(128)}, ...), condition=%wide.region_48.49_spmd.clone, body=%wide.region_47.48_spmd.clone.sunk | while | flops 983072 | bytes 1966495 | solution.py:96
  1205.8 24.5 %all-gather.17 = bf16[16,1,24]{2,1,0:T(2,128)(2,1)S(1)} all-gather(bf16[1,1,24]{2,1,0:T(2,128)(2,1)} %get-tuple-element.1025), channel_id=1, replica_groups=mesh['section'=2,'fsdp'=16,'rep'=4] {'fsdp'}, dimensions={0}, use_global_device_ids=true | all-gather | bytes 816 | tf_op jit(solution)/shard_map/all_gather | solution.py:80
  1305.1 30.3 %while.89 = (s32[]{:T(128)}, f32[24,64,128]{2,1,0:T(8,128)S(1)}, s32[]{:T(128)}, bf16[16,24]{1,0:T(8,128)(2,1)}, bf16[16,24,64,128]{3,2,1,0:T(8,128)(2,1)}, /*index=5*/s32[]{:T(128)}, s32[]{:T(128)}, s32[]{:T(128)}, s32[]{:T(128)}) while((s32[]{:T(128)}, f32[24,64,128]{2,1,0:T(8,128)S(1)}, s32[]{:T(128)}, ...), condition=%wide.region_66.67_spmd.clone, body=%wide.region_65.66_spmd.clone.sunk | while | flops 983072 | bytes 1966495 | solution.py:96
  1366.2 7.0 convolution_convert_fusion.1
  1373.2 7.5 pad_maximum_fusion
  1416.9 68.1 %reduce-scatter.11.cloned.1.call-done = bf16[64,4120]{1,0:T(8,128)(2,1)} async-done(((bf16[1024,4120]{1,0:T(8,128)(2,1)}), bf16[64,4120]{1,0:T(8,128)(2,1)}) %reduce-scatter.11.cloned.1.call-update) | async-done | bytes 527376 | tf_op jit(solution)/shard_map/reduce_scatter | solution.py:113
  1486.8 81.0 %reduce-scatter.13.cloned.1.call-done = bf16[128,1024]{1,0:T(8,128)(2,1)} async-done(((bf16[2048,1024]{1,0:T(8,128)(2,1)}), bf16[128,1024]{1,0:T(8,128)(2,1)}) %reduce-scatter.13.cloned.1.call-update) | async-done | bytes 262160 | tf_op jit(solution)/shard_map/reduce_scatter | solution.py:740
  1567.8 83.6 %reduce-scatter.17.cloned.1.call-done = bf16[128,1024]{1,0:T(8,128)(2,1)} async-done(((bf16[2048,1024]{1,0:T(8,128)(2,1)}), bf16[128,1024]{1,0:T(8,128)(2,1)}) %reduce-scatter.17.cloned.1.call-update) | async-done | bytes 262160 | tf_op jit(solution)/shard_map/reduce_scatter | solution.py:746
  1651.4 105.8 %reduce-scatter.15.cloned.1.call-done = bf16[64,4096]{1,0:T(8,128)(2,1)} async-done(((bf16[1024,4096]{1,0:T(8,128)(2,1)}), bf16[64,4096]{1,0:T(8,128)(2,1)}) %reduce-scatter.15.cloned.1.call-update) | async-done | bytes 524304 | tf_op jit(solution)/shard_map/reduce_scatter | solution.py:743
  1758.0 60.7 %all-reduce.54 = (bf16[16,3,24]{2,1,0:T(4,128)(2,1)S(1)}, bf16[1792]{0:T(1024)(128)(2,1)S(1)}) all-reduce(bf16[16,3,24]{2,1,0:T(4,128)(2,1)S(1)} %broadcast_in_dim.630, bf16[1792]{0:T(1024)(128)(2,1)S(1)} %add_convert_fusion.16), channel_id=18, replica_groups=mesh['section'=2,'fsdp'=16,'rep'=4] {'fsdp'}, use_global_device_ids=true, to_apply=%region_125.126.clone | all-reduce | flops 2944 | bytes 11776
  1824.0 66.7 %reduce-scatter.19.cloned.1.call-done = bf16[64,2]{1,0:T(8,128)(2,1)} async-done(((bf16[1024,2]{1,0:T(8,128)(2,1)}), bf16[64,2]{1,0:T(8,128)(2,1)}) %reduce-scatter.19.cloned.1.call-update) | async-done | bytes 272
  1892.3 13.4 all-reduce.55
  1908.5 36.8 %all-reduce.59.cloned.1.call-done = (bf16[1,64,4096]{2,1,0:T(8,128)(2,1)}, bf16[1,128,1024]{2,1,0:T(8,128)(2,1)}, bf16[1,64,4096]{2,1,0:T(8,128)(2,1)}, bf16[1,128,1024]{2,1,0:T(8,128)(2,1)}) async-done(((bf16[1,64,4096]{2,1,0:T(8,128)(2,1)}, bf16[1,128,1024]{2,1,0:T(8,128)(2,1)}, bf16[1,64,4096]{2,1,0:T(8,128)(2,1)}, bf16[1,128,1024]{2,1,0:T(8,128)(2,1)}), (bf16[1,64,4096]{2,1,0:T(8,128)(2,1)}, ...) | async-done | bytes 1572880 | tf_op jit(solution)/shard_map/psum | solution.py:765
  (1414 shorter events, 846.3 us)
Async XLA Ops:
  7.2 142.7 %all-gather.29.cloned.1.call-start = ((), (), s32[]{:S(2)}) async-start(), calls=%async_computation.12 | async-start | bytes 9191424 | tf_op jit(solution)/shard_map/all_gather | solution.py:102
  10.0 224.1 %all-gather.31.cloned.1.call-start = ((), (), s32[]{:S(2)}) async-start(), calls=%async_computation.17 | async-start | bytes 6684672 | tf_op jit(solution)/shard_map/all_gather | solution.py:60
  164.8 126.1 %all-gather.33.cloned.1.call-start = ((), (), s32[]{:S(2)}) async-start(), calls=%async_computation.18 | async-start | bytes 4456448 | tf_op jit(solution)/shard_map/all_gather | solution.py:628
  165.5 199.1 %all-gather.35.cloned.1.call-start = ((), (), s32[]{:S(2)}) async-start(), calls=%async_computation.19 | async-start | bytes 8912896 | tf_op jit(solution)/shard_map/all_gather | solution.py:629
  166.1 254.6 %all-gather.37.cloned.1.call-start = ((), (), s32[]{:S(2)}) async-start(), calls=%async_computation.20 | async-start | bytes 4456448 | tf_op jit(solution)/shard_map/all_gather | solution.py:630
  174.5 35.1 %all-to-all-start = ((bf16[16,64,256]{2,1,0:T(8,128)(2,1)}), bf16[16,64,256]{2,1,0:T(8,128)(2,1)S(1)}, u32[]{:S(2)}, u32[]{:S(2)}) async-start(bf16[16,64,256]{2,1,0:T(8,128)(2,1)} %broadcast_in_dim.581), calls=%async_computation | async-start | bytes 1048576 | tf_op jit(solution)/shard_map/all_to_all | solution.py:44
  181.0 340.5 %all-gather.39.cloned.1.call-start = ((), (), s32[]{:S(2)}) async-start(), calls=%async_computation.21 | async-start | bytes 6684672 | tf_op jit(solution)/shard_map/all_gather | solution.py:60
  423.7 4.9 collective-permute-start.1
  437.3 4.9 collective-permute-start.2
  453.1 37.1 %all-to-all-start.1 = ((bf16[16,64,256]{2,1,0:T(8,128)(2,1)}), bf16[16,64,256]{2,1,0:T(8,128)(2,1)}, u32[]{:S(2)}, u32[]{:S(2)}) async-start(bf16[16,64,256]{2,1,0:T(8,128)(2,1)} %broadcast_in_dim.588), calls=%async_computation.1 | async-start | bytes 1048576 | tf_op jit(solution)/shard_map/all_to_all | solution.py:44
  461.3 187.0 %all-gather.41.cloned.1.call-start = ((), (), s32[]{:S(2)}) async-start(), calls=%async_computation.22 | async-start | bytes 6684672 | tf_op jit(solution)/shard_map/all_gather | solution.py:60
  538.4 5.1 collective-permute-start.3
  548.4 5.7 collective-permute-start.4
  573.8 57.7 %all-to-all-start.2 = ((bf16[16,64,256]{2,1,0:T(8,128)(2,1)}), bf16[16,64,256]{2,1,0:T(8,128)(2,1)S(1)}, u32[]{:S(2)}, u32[]{:S(2)}) async-start(bf16[16,64,256]{2,1,0:T(8,128)(2,1)} %broadcast_in_dim.591), calls=%async_computation.2 | async-start | bytes 1048576 | tf_op jit(solution)/shard_map/all_to_all | solution.py:44
  595.4 243.2 %all-gather.43.cloned.1.call-start = ((), (), s32[]{:S(2)}) async-start(), calls=%async_computation.23 | async-start | bytes 6684672 | tf_op jit(solution)/shard_map/all_gather | solution.py:80
  808.6 18.6 all-to-all-start.3
  813.0 264.9 %all-gather.45.cloned.1.call-start = ((), (), s32[]{:S(2)}) async-start(), calls=%async_computation.24 | async-start | bytes 6684672 | tf_op jit(solution)/shard_map/all_gather | solution.py:80
  913.4 5.3 collective-permute-start.5
  928.9 5.8 collective-permute-start.6
  1049.4 17.2 all-to-all-start.4
  1053.6 251.5 %all-gather.47.cloned.1.call-start = ((), (), s32[]{:S(2)}) async-start(), calls=%async_computation.25 | async-start | bytes 6684672 | tf_op jit(solution)/shard_map/all_gather | solution.py:80
  1152.7 5.3 collective-permute-start.7
  1168.2 5.7 collective-permute-start.8
  1281.2 15.9 all-to-all-start.5
  1285.5 199.4 %reduce-scatter.11.cloned.1.call-start = ((), (), s32[]{:S(2)}) async-start(), calls=%async_computation.13 | async-start | bytes 9191424 | tf_op jit(solution)/shard_map/reduce_scatter | solution.py:113
  1360.0 5.3 collective-permute-start.9
  1380.8 187.0 %reduce-scatter.13.cloned.1.call-start = ((), (), s32[]{:S(2)}) async-start(), calls=%async_computation.14 | async-start | bytes 4456448 | tf_op jit(solution)/shard_map/reduce_scatter | solution.py:740
  1385.5 265.9 %reduce-scatter.17.cloned.1.call-start = ((), (), s32[]{:S(2)}) async-start(), calls=%async_computation.16 | async-start | bytes 4456448 | tf_op jit(solution)/shard_map/reduce_scatter | solution.py:746
  1392.4 364.9 %reduce-scatter.15.cloned.1.call-start = ((), (), s32[]{:S(2)}) async-start(), calls=%async_computation.15 | async-start | bytes 8912896 | tf_op jit(solution)/shard_map/reduce_scatter | solution.py:743
  1400.3 421.8 %reduce-scatter.21.cloned.1.call-start = ((), (), s32[]{:S(2)}) async-start(), calls=%async_computation.27 | async-start | bytes 487424
  1408.0 482.7 %reduce-scatter.19.cloned.1.call-start = ((), (), s32[]{:S(2)}) async-start(), calls=%async_computation.26 | async-start | bytes 278528
  1416.8 528.5 %all-reduce.59.cloned.1.call-start = ((), (), s32[]{:S(2)}) async-start(), calls=%async_computation.28 | async-start | bytes 3145728 | tf_op jit(solution)/shard_map/psum | solution.py:765
  (317 other events, 9058.5 us)
Sparse Core Ops, SparseCore 0:
  11.0 79.5 all-gather.28
  164.9 69.1 all-gather.30
  236.5 54.3 all-gather.32
  293.1 71.4 all-gather.34
  366.9 53.7 all-gather.36
  448.6 72.8 all-gather.38
  564.3 83.9 all-gather.40
  696.8 79.8 all-gather.42
  966.7 66.3 all-gather.44
  1205.9 66.3 all-gather.46
  1380.9 104.0 reduce-scatter.10
  1488.9 78.8 reduce-scatter.12
  1572.4 78.9 reduce-scatter.16
  1655.6 101.5 reduce-scatter.14
  1761.3 60.7 reduce-scatter.20
  1826.7 63.9 reduce-scatter.18
  1893.7 51.5 all-reduce.58
where the time goes:
time: 1980 us; the launch traced here: 1960 us
  waiting for transfers between devices  701 us (35%)
  blocking collectives  325 us (16%)
  local copies, waits for them, and re-layouts  281 us (14%)
  other arithmetic  280 us (14%)
  matrix products  266 us (13%)
  starting transfers between devices  78.4 us (4%)
  between operations  24.5 us (1%)
    reduce_scatter x1, waiting for transfers between devices, local(): lax.psum_scatter(grad_gate_up_weight.astype(jnp.bfloat16), 'fsdp', scatte...  106 us
    unnamed x2, blocking collectives  94 us
    all_gather x3, blocking collectives, carried_in(): lax.all_gather(part.astype(kind), axis)  86 us
    reduce_scatter x1, waiting for transfers between devices, local(): lax.psum_scatter(grad_down_weight.astype(jnp.bfloat16), 'fsdp', scatter_d...  83.6 us
    reduce_scatter x1, waiting for transfers between devices, local(): lax.psum_scatter(grad_out_weight.astype(jnp.bfloat16), 'fsdp', scatter_di...  81 us
    all_gather x3, blocking collectives, entering(): lax.all_gather(a.astype(kind), axis)  78.6 us
    unnamed x19, waiting for transfers between devices  71.4 us
    all_gather x1, waiting for transfers between devices, local(): lax.all_gather(w_gate_up[0], 'fsdp', axis=0, tiled=True)  69.9 us
  transfers between devices with their start and end apart: 33, of which 23 were waited for; matrix products, arithmetic and copies ran while one was open for 21% of the time, Pallas kernels for 0%

commit v1 on v0

v1 whole, which is shorter than its diff:
```python
import jax
import jax.numpy as jnp
import numpy as np
from jax import lax
from jax.experimental import pallas as pl
from jax.experimental.pallas import tpu as pltpu
from jax.sharding import Mesh
from jax.sharding import PartitionSpec as P

QUERY_HEADS = 8
KEY_VALUE_HEADS = 2
HEAD_SIZE = 64
MIXER_HEADS = 24
STATE_SIZE = 128
KC = 4
FF = 2048
SPACE_CHANNELS = 1536
XBC = 1792
BLOCK = 64

TEAM = 8
HALVES = 2
HEADS = MIXER_HEADS // TEAM
CH = SPACE_CHANNELS // TEAM
CONV = CH + 2 * STATE_SIZE
SEQ = 512
COLS = 896
STEP_AT = 2 * CH + 2 * STATE_SIZE + 3 * HEAD_SIZE
SMALL_AT = STEP_AT + HEADS
HID = FF // TEAM

rope_base = 100000000000.0
norm_epsilon = 1e-05
masked_score = -1e30
bf = jnp.bfloat16
f32 = jnp.float32


def mm(left, right):
    return jnp.dot(left, right, preferred_element_type=f32)


def mm_t(left, right):
    return lax.dot_general(left, right, (((1,), (1,)), ((), ())), preferred_element_type=f32)


def t_mm(left, right):
    return lax.dot_general(left, right, (((0,), (0,)), ((), ())), preferred_element_type=f32)


def after(x, *others):
    return lax.optimization_barrier((x, others))[0]


def shifted(x, axis, by, devices):
    return lax.ppermute(x, axis, [(i, (i + by) % devices) for i in range(devices)])


def swap(x, axis):
    return lax.ppermute(x, axis, [(0, 1), (1, 0)])


def gather_ring(x, axis):
    devices = 4
    parts = jnp.stack([x] + [shifted(x, axis, by, devices) for by in range(1, devices)])
    order = (lax.axis_index(axis) - jnp.arange(devices)) % devices
    return parts[order]


RING = ("section", "zhi")
FORWARD = [(0, 2), (2, 1), (1, 3), (3, 0)]
BACKWARD = [(b, a) for a, b in FORWARD]


def around(x):
    half = x.shape[0] // 2
    behind = lax.ppermute(x, RING, FORWARD)
    ahead = lax.ppermute(x, RING, BACKWARD)
    far = (
        lax.ppermute(behind[:half], RING, FORWARD),
        lax.ppermute(ahead[half:], RING, BACKWARD),
    )
    return x, jnp.concatenate(far), behind, ahead


def place_of_unit(unit):
    return (unit, 0) if unit < 8 else ((unit - 8) // 3, 1 + (unit - 8) % 3)


def unit_routes():
    edges = []
    for unit in range(32):
        team, slot = place_of_unit(unit)
        for half in range(2):
            edges.append((unit // 2, half * 8 + team, unit % 2, slot))
    routes = []
    left = list(edges)
    while left:
        taken = {}

        def place(source, seen):
            for e in left:
                if e[0] != source or e[1] in seen:
                    continue
                seen.add(e[1])
                if e[1] not in taken or place(taken[e[1]][0], seen):
                    taken[e[1]] = e
                    return True
            return False

        for source in range(16):
            place(source, set())
        chosen = sorted(taken.values())
        routes.append(chosen)
        for e in chosen:
            left.remove(e)
    return routes


ROUTES = unit_routes()
UNIT_AXES = ("zhi", "y", "core")


def device_table():
    table = np.zeros((16, 30), np.int32)
    for at in range(16):
        table[at, :3] = (at % 8) // 2, at % 2, at // 8
    for r, route in enumerate(ROUTES):
        for source, dest, unit, slot in route:
            table[source, 4 + r] = unit
            table[dest, 8 + r] = slot
    for at in range(16):
        half, member = at // 8, at % 8
        for other in range(8):
            for k in range(2):
                team, slot = place_of_unit(2 * (8 * half + other) + k)
                table[at, 12 + 2 * other + k] = slot if team == member else 0
        for k in range(2):
            table[at, 28 + k] = place_of_unit(2 * at + k)[0]
    return table


def device_info():
    at = lax.axis_index(UNIT_AXES).astype(jnp.uint32)
    return lax.dynamic_slice(jnp.asarray(device_table()), (at, jnp.uint32(0)), (1, 30)).reshape(30)


def pick_units_kernel(info, w, *outs):
    for r, out in enumerate(outs):
        out[...] = w[info[4 + r]]


def place_units_kernel(info, g0, g1, g2, g3, out):
    for r, got in enumerate((g0, g1, g2, g3)):
        out[info[8 + r]] = got[...]


def send_early_kernel(info, half, more, out):
    for member in range(TEAM):
        out[member, :UP_TILES] = half[member * UP_TILES : (member + 1) * UP_TILES]
        for k in range(2):
            at = UP_TILES + 8 * k
            out[member, at : at + 8] = more[info[12 + 2 * member + k]]


def got_early_kernel(info, got, half, out):
    for member in range(TEAM):
        out[member * UP_TILES : (member + 1) * UP_TILES] = got[member, :UP_TILES]
    at = TEAM * UP_TILES
    out[at : at + DOWN_TILES] = half[at : at + DOWN_TILES]
    for k in range(2):
        first = at + DOWN_TILES + 8 * k
        out[first : first + 8] = got[info[28 + k], UP_TILES + 8 * k : UP_TILES + 8 * (k + 1)]


def spread_units(w, info):
    pieces = call(pick_units_kernel, [(w.shape[1:], bf)] * 4, [], info, w)
    got = [
        lax.ppermute(piece, UNIT_AXES, [(e[0], e[1]) for e in route])
        for piece, route in zip(pieces, ROUTES)
    ]
    return call(place_units_kernel, [((4, *w.shape[1:]), bf)], [], info, *got)[0]


def pack_layout(lengths_row, count_of_blocks, rows_per_block):
    used_blocks = (lengths_row + rows_per_block - 1) // rows_per_block
    first_block = jnp.cumsum(used_blocks) - used_blocks
    block_order = jnp.arange(count_of_blocks, dtype=jnp.int32)
    covers = (
        (block_order[:, None] >= first_block[None, :])
        & (block_order[:, None] < (first_block + used_blocks)[None, :])
    ).astype(jnp.int32)
    occupied = jnp.sum(covers, axis=1) > 0
    slot_order = jnp.arange(lengths_row.shape[0], dtype=jnp.int32)
    segment = jnp.where(occupied, jnp.sum(covers * slot_order[None, :], axis=1), -1)
    begins = jnp.sum(covers * first_block[None, :], axis=1)
    seq_length = jnp.sum(covers * lengths_row[None, :], axis=1)
    within = (block_order - begins)[:, None] * rows_per_block + jnp.arange(
        rows_per_block, dtype=jnp.int32
    )[None, :]
    is_valid = occupied[:, None] & (within < seq_length[:, None])
    carry_flag = occupied & (block_order > begins)
    return (segment, within, is_valid, carry_flag)


def facts(lengths_row, half, team):
    segment, within, is_valid, carry = pack_layout(lengths_row, 2 * TEAM, BLOCK)
    start = half * SEQ

    def mine(x):
        return lax.dynamic_slice_in_dim(x, start, SEQ, 0)

    seg_rows = jnp.repeat(segment, BLOCK)
    chain = jnp.cumsum(1 - carry.astype(jnp.int32))
    chain_rows = mine(jnp.repeat(chain, BLOCK))
    carry_rows = mine(jnp.repeat(carry, BLOCK)).astype(f32)
    position = mine(within.reshape(-1))
    valid = is_valid.reshape(-1)
    own_valid = lax.dynamic_slice_in_dim(valid, start + team * BLOCK, BLOCK, 0)
    half_width = HEAD_SIZE // 2
    frequency = rope_base ** (-jnp.arange(half_width, dtype=f32) / half_width)
    angles = position.astype(f32)[:, None] * frequency[None, :]
    cos, sin = jnp.cos(angles), jnp.sin(angles)
    enters = ((chain_rows == chain_rows[0]) & (carry_rows[0] > 0)).astype(f32)
    leaves = (chain_rows == chain_rows[SEQ - 1]).astype(f32)
    key_seg = jnp.where(valid, seg_rows, -2).astype(f32)
    columns = [mine(seg_rows).astype(f32), chain_rows.astype(f32), enters, leaves, carry_rows]
    rows = [mine(key_seg), jnp.where(half == 1, key_seg[:SEQ], -3.0), chain_rows.astype(f32)]
    return dict(
        trig=jnp.concatenate([cos, cos, cos, cos, -sin, sin, -sin, sin], axis=1),
        valid=own_valid.astype(f32)[:, None],
        rowf=jnp.pad(jnp.stack(columns, axis=1), ((0, 0), (0, 128 - len(columns)))),
        colf=jnp.pad(jnp.stack(rows), ((0, 8 - len(rows)), (0, 0))),
        info=device_info(),
        half=half,
    )


def norm(x, gain):
    r = lax.rsqrt(jnp.mean(x * x, axis=-1, keepdims=True) + norm_epsilon)
    return x * r * gain, r


def norm_back(grad, x, r, gain):
    e = grad * gain
    gx = r * e - x * (r * r * r) * jnp.mean(x * e, axis=-1, keepdims=True)
    return gx


def half_first(x):
    middle = x.shape[1] // 2
    turned = jnp.concatenate([x[:, middle:], x[:, :middle]], axis=1)
    return jnp.where(lax.axis_index("zhi") == 0, x, turned)


def to_first(x):
    return lax.ppermute(x, "zhi", [(1, 0)])


ROWS = 128
STEPS = SEQ // ROWS
B_AT, C_AT, X_AT, Z_AT, Q_AT, V_AT = 0, 128, 256, 448, 640, 768
PACKED = SEQ + CH + 64
PAD = 16
LANE = 64


def nt(left, right):
    return lax.dot_general(left, right, (((1,), (1,)), ((), ())), preferred_element_type=f32)


def tn(left, right):
    return lax.dot_general(left, right, (((0,), (0,)), ((), ())), preferred_element_type=f32)


def exact(left, right):
    return jnp.dot(left, right, precision=lax.Precision.HIGHEST, preferred_element_type=f32)


def iota(shape, axis):
    return lax.broadcasted_iota(jnp.int32, shape, axis)


def head(x, k):
    return x[:, k * HEAD_SIZE : (k + 1) * HEAD_SIZE]


def lane(x, k):
    return x[:, LANE + k : LANE + k + 1]


def on_lanes(columns):
    at = iota((columns[0].shape[0], 128), 1)
    total = jnp.zeros((columns[0].shape[0], 128), f32)
    for k, column in enumerate(columns):
        total = jnp.where(at == LANE + k, column, total)
    return total


def assemble(info, pieces, others, rows):
    y, core = info[0], info[1]
    for back in range(4):
        at = ((y - back) & 3) * ROWS
        rows[pl.ds(pl.multiple_of(at + core * BLOCK, BLOCK), BLOCK), :] = pieces[back][...]
        rows[pl.ds(pl.multiple_of(at + (1 - core) * BLOCK, BLOCK), BLOCK), :] = others[back]


def deliver(info, value, step, mine, other):
    first = info[1] == 0
    to = (step - info[0]) & 3
    upper, lower = value[:BLOCK].astype(bf), value[BLOCK:].astype(bf)
    mine[to] = jnp.where(first, upper, lower)
    other[to] = jnp.where(first, lower, upper)


def swapped_halves(x):
    q = HEAD_SIZE // 2
    return jnp.concatenate([x[:, q : 2 * q], x[:, :q], x[:, 3 * q :], x[:, 2 * q : 3 * q]], axis=1)


def tap_mask(rowf, at, tap):
    within = iota((ROWS, 1), 0) & (BLOCK - 1)
    return jnp.where(within + tap >= KC - 1, 1.0, rowf[at : at + ROWS, 4:5])


def tap_rows(pad, rowf, at, tap):
    first = PAD - (KC - 1) + tap + at
    return pad[first : first + ROWS, :] * tap_mask(rowf, at, tap)


def conv_pre(pad, rowf, cw, at):
    pre = cw[4:5, :]
    for tap in range(KC):
        pre = pre + cw[tap : tap + 1, :] * tap_rows(pad, rowf, at, tap)
    return pre


def fill_pad(pad, mixed, edge):
    if edge is None:
        pad[:PAD, :] = jnp.zeros((PAD, CONV), f32)
    else:
        at = SEQ + CH
        whole = jnp.concatenate([edge[at + 16 * k : at + 16 * (k + 1), :] for k in range(4)], axis=1)
        pad[:PAD, :] = whole[:, :CONV].astype(f32)
    for at in range(0, SEQ, ROWS):
        pad[PAD + at : PAD + at + ROWS, :] = mixed[at : at + ROWS, :CONV].astype(bf).astype(f32)


def write_edge(out, rows):
    at = SEQ + CH
    for k in range(4):
        out[at + 16 * k : at + 16 * (k + 1), :] = rows[:, 128 * k : 128 * (k + 1)].astype(bf)


def mix_kernel(
    info, p0, p1, p2, p3, others, gains, wm, trig, rowf, cw, hv, rows, mixed, cs, qkv, pack, pad, raw
):
    assemble(info, (p0, p1, p2, p3), others, raw)
    middle = raw.shape[1] // 2
    lower = (iota((ROWS, ROWS), 0) >= iota((ROWS, ROWS), 1)).astype(f32)
    base = jnp.zeros((1, 128), f32)
    low_lanes = iota((ROWS, 128), 1) < HEAD_SIZE
    for at in range(0, SEQ, ROWS):
        r = slice(at, at + ROWS)
        x = raw[r, :].astype(f32)
        root = lax.rsqrt(jnp.mean(x * x, axis=1, keepdims=True) + norm_epsilon)
        n = (x * root * gains[0:1, :]).astype(bf)
        turned = jnp.concatenate([n[:, middle:], n[:, :middle]], axis=1)
        n = jnp.where(info[2] == 0, n, turned)
        rows[r, :] = n
        m = jnp.dot(n, wm[...], preferred_element_type=f32)
        mixed[r, :] = m
        qk = m[:, Q_AT:V_AT]
        qk = qk * trig[r, :128] + swapped_halves(qk) * trig[r, 128:]
        last = m[:, V_AT:]
        qkv[r, :128] = qk.astype(bf)
        qkv[r, 128:] = last.astype(bf)
        pack[r, :] = jnp.where(low_lanes, last, qk).astype(bf)
        step = jax.nn.softplus(last + hv[0:1, :])
        cum = exact(lower, step * hv[1:2, :]) + base
        base = cum[ROWS - 1 :, :]
        cs[r, :128] = cum
        cs[r, 128:] = step
    fill_pad(pad, mixed, None)
    state = jnp.zeros((CH, STATE_SIZE), f32)
    for at in range(0, SEQ, ROWS):
        r = slice(at, at + ROWS)
        act = jax.nn.silu(conv_pre(pad, rowf, cw, at))
        scale = jnp.exp(base - cs[r, :128]) * cs[r, 128:] * rowf[r, 3:4]
        scaled = jnp.concatenate(
            [head(act[:, X_AT:], k) * lane(scale, k) for k in range(HEADS)], axis=1
        )
        state = state + tn(scaled.astype(bf), act[:, B_AT:C_AT].astype(bf))
    pack[SEQ : SEQ + CH, :] = state.astype(bf)
    write_edge(pack, mixed[SEQ - 16 :, :512])


def own_scores(qkv, colf, rowf, at):
    n = at + ROWS
    s = nt(qkv[at:n, :HEAD_SIZE], qkv[:n, HEAD_SIZE : 2 * HEAD_SIZE]) * HEAD_SIZE**-0.5
    row, col = at + iota((ROWS, n), 0), iota((ROWS, n), 1)
    ok = ((rowf[at:n, 0:1] == colf[0:1, :n]) & (col <= row)) | (col == row)
    return jnp.where(ok, s, masked_score)


def other_scores(qkv, got, colf, rowf, at):
    r = slice(at, at + ROWS)
    s = nt(qkv[r, :HEAD_SIZE], got[:SEQ, HEAD_SIZE:]) * HEAD_SIZE**-0.5
    return jnp.where(rowf[r, 0:1] == colf[1:2, :], s, masked_score)


def decay_of(cs, cum_t, linked, at, k):
    n = at + ROWS
    gap = cs[at:n, LANE + k : LANE + k + 1] - cum_t[LANE + k : LANE + k + 1, :n]
    return jnp.where(linked, jnp.exp(jnp.minimum(gap, 0.0)), 0.0)


def linked_rows(rowf, colf, at):
    n = at + ROWS
    row, col = at + iota((ROWS, n), 0), iota((ROWS, n), 1)
    return (rowf[at:n, 1:2] == colf[2:3, :n]) & (col <= row)


def head_kernel(
    info, mixed, cs, qkv, got, wout, rowf, colf, cw, hv, mine, other, joined, ssm_out, stats,
    pad, act, cum_t, step_t,
):
    fill_pad(pad, mixed, got)
    cum_t[...] = cs[:, :128].T
    step_t[...] = cs[:, 128:].T
    for at in range(0, SEQ, ROWS):
        r, n = slice(at, at + ROWS), at + ROWS
        own = own_scores(qkv, colf, rowf, at)
        far = other_scores(qkv, got, colf, rowf, at)
        peak = jnp.maximum(
            jnp.max(own, axis=1, keepdims=True), jnp.max(far, axis=1, keepdims=True)
        )
        own, far = jnp.exp(own - peak), jnp.exp(far - peak)
        total = jnp.sum(own, axis=1, keepdims=True) + jnp.sum(far, axis=1, keepdims=True)
        stats[r, :] = jnp.broadcast_to(peak + jnp.log(total), (ROWS, 128))
        scale = 1.0 / total
        attended = mm((own * scale).astype(bf), qkv[:n, 128 : 128 + HEAD_SIZE]) + mm(
            (far * scale).astype(bf), got[:SEQ, :HEAD_SIZE]
        )
        a = jax.nn.silu(conv_pre(pad, rowf, cw, at))
        act[r, :] = a.astype(bf)
        c_low = act[r, C_AT:X_AT]
        meet = nt(c_low, act[:n, B_AT:C_AT])
        linked = linked_rows(rowf, colf, at)
        carried = nt(c_low, got[SEQ : SEQ + CH, :])
        in_scale = jnp.exp(cs[r, :128]) * rowf[r, 2:3]
        outs = []
        for k in range(HEADS):
            weights = meet * decay_of(cs, cum_t, linked, at, k) * step_t[LANE + k : LANE + k + 1, :n]
            x_at = X_AT + k * HEAD_SIZE
            outs.append(
                mm(weights.astype(bf), act[:n, x_at : x_at + HEAD_SIZE])
                + lane(in_scale, k) * head(carried, k)
                + hv[2:3, LANE + k : LANE + k + 1] * head(a[:, X_AT:], k)
            )
        ssm = jnp.concatenate(outs, axis=1)
        ssm_out[r, :] = ssm
        j = jnp.concatenate([attended, ssm * jax.nn.silu(mixed[r, Z_AT:Q_AT])], axis=1).astype(bf)
        joined[r, :] = j
        deliver(info, mm(j, wout[...]), at // ROWS, mine, other)


def ffn_kernel(info, p0, p1, p2, p3, others, wup, wdown, rows, gate_up, hidden, mine, other):
    assemble(info, (p0, p1, p2, p3), others, rows)
    for at in range(0, SEQ, ROWS):
        r = slice(at, at + ROWS)
        gu = mm(rows[r, :], wup[...])
        gate_up[r, :] = gu
        h = (jax.nn.silu(gu[:, :HID]) * gu[:, HID:]).astype(bf)
        hidden[r, :] = h
        deliver(info, mm(h, wdown[...]), at // ROWS, mine, other)


def slope(z):
    s = jax.nn.sigmoid(z)
    return s * (1.0 + z * (1.0 - s))


def half_order(info, row):
    middle = row.shape[1] // 2
    turned = jnp.concatenate([row[:, middle:], row[:, :middle]], axis=1)
    return jnp.where(info[2] == 0, row, turned)


def ffn_back_kernel(
    info, p0, p1, p2, p3, others, wup, wdown, gate_up, normed, gains,
    rows, grad_up, mine, other, g_gain,
):
    assemble(info, (p0, p1, p2, p3), others, rows)
    total = jnp.zeros((1, rows.shape[1]), f32)
    for at in range(0, SEQ, ROWS):
        r = slice(at, at + ROWS)
        gh = nt(rows[r, :], wdown[...])
        gate, up = gate_up[r, :HID], gate_up[r, HID:]
        g = jnp.concatenate([gh * up * slope(gate), gh * jax.nn.silu(gate)], axis=1).astype(bf)
        grad_up[r, :] = g
        back = nt(g, wup[...])
        total = total + jnp.sum(back * normed[r, :].astype(f32), axis=0, keepdims=True)
        deliver(info, back, at // ROWS, mine, other)
    g_gain[...] = jnp.broadcast_to(total / half_order(info, gains[1:2, :]), g_gain.shape)


def head_back_kernel(
    info, p0, p1, p2, p3, others, wout, mixed, cs, qkv, got, ssm, stats, rowf, colf, cw, hv,
    rows, g_act, g_cs, g_qkv, g_z, send, g_skip,
    pad, act, cum_t, step_t, own_t, far_t, act_t, column,
):
    assemble(info, (p0, p1, p2, p3), others, rows)
    fill_pad(pad, mixed, got)
    cum_t[...] = cs[:, :128].T
    step_t[...] = cs[:, 128:].T
    own_t[...] = jnp.zeros((128, SEQ), f32)
    far_t[...] = jnp.zeros((128, SEQ), f32)
    act_t[...] = jnp.zeros((128 + CH, SEQ), f32)
    column[...] = jnp.zeros((128, SEQ), f32)
    state_t = jnp.zeros((STATE_SIZE, CH), f32)
    skips = [jnp.zeros((1, 1), f32) for _ in range(HEADS)]
    for at in range(0, SEQ, ROWS):
        r, n = slice(at, at + ROWS), at + ROWS
        a = jax.nn.silu(conv_pre(pad, rowf, cw, at))
        act[r, :] = a.astype(bf)
        gj = nt(rows[r, :], wout[...])
        g_att = gj[:, :HEAD_SIZE].astype(bf)
        gated = gj[:, HEAD_SIZE:]
        z = mixed[r, Z_AT:Q_AT]
        g_ssm = gated * jax.nn.silu(z)
        g_z[r, :] = gated * ssm[r, :] * slope(z)
        lse = stats[r, 0:1]
        p_own = jnp.exp(own_scores(qkv, colf, rowf, at) - lse)
        p_far = jnp.exp(other_scores(qkv, got, colf, rowf, at) - lse)
        g_own = nt(g_att, qkv[:n, 128 : 128 + HEAD_SIZE])
        g_far = nt(g_att, got[:SEQ, :HEAD_SIZE])
        total = jnp.sum(p_own * g_own, axis=1, keepdims=True) + jnp.sum(
            p_far * g_far, axis=1, keepdims=True
        )
        s_own = (p_own * (g_own - total) * HEAD_SIZE**-0.5).astype(bf)
        s_far = (p_far * (g_far - total) * HEAD_SIZE**-0.5).astype(bf)
        query = qkv[r, :HEAD_SIZE].astype(f32)
        g_qkv[r, :HEAD_SIZE] = mm(s_own, qkv[:n, HEAD_SIZE : 2 * HEAD_SIZE]) + mm(
            s_far, got[:SEQ, HEAD_SIZE:]
        )
        turned = jnp.concatenate([gj[:, :HEAD_SIZE], query], axis=1).T.astype(bf)
        att_t, query_t = turned[:HEAD_SIZE], turned[HEAD_SIZE:]
        own_t[:HEAD_SIZE, :n] += mm(att_t, p_own.astype(bf))
        own_t[HEAD_SIZE:, :n] += mm(query_t, s_own)
        far_t[:HEAD_SIZE, :] += mm(att_t, p_far.astype(bf))
        far_t[HEAD_SIZE:, :] += mm(query_t, s_far)
        c_low = act[r, C_AT:X_AT]
        meet = nt(c_low, act[:n, B_AT:C_AT])
        linked = linked_rows(rowf, colf, at)
        state = got[SEQ : SEQ + CH, :]
        carried = nt(c_low, state)
        in_scale = jnp.exp(cs[r, :128]) * rowf[r, 2:3]
        g_meet = jnp.zeros((ROWS, n), f32)
        g_carried, g_cum = [], []
        turned = jnp.concatenate([a[:, C_AT:X_AT], g_ssm, jnp.zeros((ROWS, 64), f32)], axis=1)
        turned = turned.T.astype(bf)
        c_t = turned[:STATE_SIZE]
        for k in range(HEADS):
            x_at = X_AT + k * HEAD_SIZE
            xk, gk = head(a[:, X_AT:], k), head(g_ssm, k)
            g_low = gk.astype(bf)
            decay = decay_of(cs, cum_t, linked, at, k)
            step_row = step_t[LANE + k : LANE + k + 1, :n]
            part = nt(g_low, act[:n, x_at : x_at + HEAD_SIZE]) * decay
            g_meet = g_meet + part * step_row
            product = part * meet
            column[LANE + k : LANE + k + 1, :n] += jnp.sum(product, axis=0, keepdims=True)
            row = jnp.sum(product * step_row, axis=1, keepdims=True)
            t_at = 128 + k * HEAD_SIZE
            act_t[t_at : t_at + HEAD_SIZE, :n] += mm(
                turned[t_at : t_at + HEAD_SIZE], (meet * decay * step_row).astype(bf)
            )
            g_act[r, x_at : x_at + HEAD_SIZE] = hv[2:3, LANE + k : LANE + k + 1] * gk
            g_scale = jnp.sum(gk * head(carried, k), axis=1, keepdims=True)
            g_cum.append(row + g_scale * lane(in_scale, k))
            g_carried.append(gk * lane(in_scale, k))
            skips[k] = skips[k] + jnp.sum(
                jnp.sum(gk * xk, axis=1, keepdims=True), axis=0, keepdims=True
            )
        g_cs[r, :128] = on_lanes(g_cum)
        g_carried = jnp.concatenate(g_carried, axis=1).astype(bf)
        g_meet = g_meet.astype(bf)
        g_act[r, C_AT:X_AT] = mm(g_meet, act[:n, B_AT:C_AT]) + mm(g_carried, state)
        act_t[:STATE_SIZE, :n] += mm(c_t, g_meet)
        state_t = state_t + mm(c_t, g_carried)
    g_act[:, B_AT:C_AT] = act_t[:STATE_SIZE, :].T
    g_act[:, X_AT:] += act_t[STATE_SIZE:, :].T
    own_kv = own_t[...].T
    g_qkv[:, HEAD_SIZE : 2 * HEAD_SIZE] = own_kv[:, HEAD_SIZE:]
    g_qkv[:, 128 : 128 + HEAD_SIZE] = own_kv[:, :HEAD_SIZE]
    g_qkv[:, 128 + HEAD_SIZE :] = jnp.zeros((SEQ, HEAD_SIZE), f32)
    turned = column[...].T
    g_cs[:, :128] = g_cs[:, :128] - turned * cs[:, 128:]
    g_cs[:, 128:] = turned
    g_skip[...] = jnp.broadcast_to(on_lanes(skips), (8, 128))
    send[:SEQ, :] = far_t[...].T.astype(bf)
    send[SEQ : SEQ + CH, :] = state_t.T.astype(bf)
    edge = g_act[:PAD, :] * slope(conv_pre(pad, rowf, cw, 0)[:PAD])
    pad[:PAD, :] = jnp.zeros((PAD, CONV), f32)
    for tap in range(KC - 1):
        first = PAD - (KC - 1) + tap
        count = PAD - first
        pad[first:PAD, :] += (
            cw[tap : tap + 1, :] * tap_mask(rowf, 0, tap)[:count] * edge[:count]
        )
    write_edge(send, jnp.concatenate([pad[:PAD, :], jnp.zeros((PAD, 64), f32)], axis=1))


def mix_back_kernel(
    info, mixed, cs, got, g_act, g_cs, g_qkv, g_z, g_skip, back, wm, trig, rowf, cw, hv,
    normed, gains, gain_two, grad, mine, other, small, pad, g_pad, acc,
):
    fill_pad(pad, mixed, got)
    total = cs[SEQ - 1 :, :128]
    state = back[SEQ : SEQ + CH, :]
    shift = jnp.zeros((1, 128), f32)
    g_pad[...] = jnp.zeros((PAD + SEQ, CONV), f32)
    kernels = [jnp.zeros((1, CONV), f32) for _ in range(KC + 1)]
    for at in range(0, SEQ, ROWS):
        r = slice(at, at + ROWS)
        pre = conv_pre(pad, rowf, cw, at)
        a = jax.nn.silu(pre)
        pulled = nt(a[:, B_AT:C_AT].astype(bf), state)
        tail = jnp.exp(total - cs[r, :128]) * rowf[r, 3:4]
        scale = tail * cs[r, 128:]
        scaled, g_x, g_scale = [], [], []
        for k in range(HEADS):
            xk, pk = head(a[:, X_AT:], k), head(pulled, k)
            g_scale.append(jnp.sum(xk * pk, axis=1, keepdims=True))
            g_x.append(pk * lane(scale, k))
            scaled.append(xk * lane(scale, k))
        g_scale = on_lanes(g_scale)
        change = g_scale * scale
        shift = shift + jnp.sum(change, axis=0, keepdims=True)
        acc[r, :128] = g_cs[r, :128] - change
        acc[r, 128:] = g_cs[r, 128:] + g_scale * tail
        g_b = mm(jnp.concatenate(scaled, axis=1).astype(bf), state)
        more = jnp.concatenate([g_b, jnp.zeros((ROWS, 128), f32), *g_x], axis=1)
        g_pre = (g_act[r, :] + more) * slope(pre)
        kernels[KC] = kernels[KC] + jnp.sum(g_pre, axis=0, keepdims=True)
        for tap in range(KC):
            kernels[tap] = kernels[tap] + jnp.sum(
                g_pre * tap_rows(pad, rowf, at, tap), axis=0, keepdims=True
            )
            first = PAD - (KC - 1) + tap + at
            g_pad[first : first + ROWS, :] += (
                cw[tap : tap + 1, :] * tap_mask(rowf, at, tap) * g_pre
            )
    edge_at = SEQ + CH
    edge = jnp.concatenate(
        [back[edge_at + 16 * k : edge_at + 16 * (k + 1), :] for k in range(4)], axis=1
    )
    g_pad[SEQ:, :] += edge[:, :CONV].astype(f32)
    upper = (iota((ROWS, ROWS), 0) <= iota((ROWS, ROWS), 1)).astype(f32)
    lanes = iota((ROWS, 128), 1)
    on_step = (lanes >= LANE) & (lanes < LANE + HEADS)
    g_bias, g_rate = jnp.zeros((1, 128), f32), jnp.zeros((1, 128), f32)
    g_gain = jnp.zeros((1, normed.shape[1]), f32)
    for at in reversed(range(0, SEQ, ROWS)):
        r = slice(at, at + ROWS)
        later = exact(upper, acc[r, :128]) + shift
        shift = later[:1, :]
        rate = hv[1:2, :]
        g_rate = g_rate + jnp.sum(later * cs[r, 128:] * rate, axis=0, keepdims=True)
        g_raw = (acc[r, 128:] + later * rate) * jax.nn.sigmoid(mixed[r, V_AT:] + hv[0:1, :])
        g_raw = jnp.where(on_step, g_raw, 0.0)
        g_bias = g_bias + jnp.sum(g_raw, axis=0, keepdims=True)
        arrived = back[r, :].astype(f32)
        qk = g_qkv[r, :128] + jnp.where(lanes >= HEAD_SIZE, arrived, 0.0)
        qk = qk * trig[r, :128] - swapped_halves(qk) * trig[r, 128:]
        last = jnp.where(lanes < HEAD_SIZE, g_qkv[r, 128:] + arrived, g_raw)
        g = jnp.concatenate([g_pad[PAD + at : PAD + at + ROWS, :], g_z[r, :], qk, last], axis=1)
        g = g.astype(bf)
        grad[r, :] = g
        g_rows = nt(g, wm[...])
        g_gain = g_gain + jnp.sum(g_rows * normed[r, :].astype(f32), axis=0, keepdims=True)
        deliver(info, g_rows, at // ROWS, mine, other)
    g_gain = g_gain / half_order(info, gains[0:1, :])
    fill = jnp.zeros((1, 64), f32)
    none = jnp.zeros((1, 128), f32)
    conv = [jnp.concatenate([k, fill], axis=1) for k in kernels]
    chunks = [
        jnp.concatenate([c[:, 128 * k : 128 * k + 128] for c in conv], axis=0) for k in range(4)
    ]
    for q in range(2):
        tile = jnp.concatenate([chunks[2 * q], chunks[2 * q + 1], *[none] * 6], axis=0).astype(bf)
        for owner in range(2 * TEAM):
            small[1 + q, owner] = tile
    heads = jnp.concatenate([g_bias, g_rate, g_skip[:1, :], *[none] * 11], axis=0)
    for owner in range(2 * TEAM):
        at = (owner % TEAM) * BLOCK + (SEQ if owner < TEAM else 0)
        own = [
            jnp.concatenate([row[:, at : at + BLOCK], fill], axis=1)
            for row in (g_gain, gain_two[:1, :])
        ]
        small[0, owner] = jnp.concatenate([*own, heads], axis=0).astype(bf)
        small[3, owner] = jnp.zeros((16, 128), bf)


UP_TILES = 2 * HID // 128
MIX_TILES = COLS // 128
DOWN_TILES = 16
EARLY = TEAM * UP_TILES + DOWN_TILES
LATE = TEAM * MIX_TILES
OUT_TILES = 32


def put_rows(out, block, at, tiles, half_tiles):
    base = half_tiles if at < SEQ else 0
    for q in range(8):
        member = (at % SEQ) // BLOCK + q // 4
        for c in range(tiles):
            tile = block[16 * q : 16 * q + 16, 128 * c : 128 * c + 128]
            out[q % 4, base + member * tiles + c] = tile


def early_kernel(info, rows_two, grad_up, hidden, grad_rows, joined, branch, out):
    width = rows_two.shape[1]
    for at in range(0, width, 128):
        block = tn(rows_two[:, at : at + 128], grad_up[...]).astype(bf)
        put_rows(out, block, at, UP_TILES, EARLY)
    for part in range(2):
        base = jnp.where(info[2] == part, EARLY, 0) + TEAM * UP_TILES
        block = tn(hidden[:, 128 * part : 128 * part + 128], grad_rows[...]).astype(bf)
        for q in range(8):
            for c in range(8):
                tile = block[16 * q : 16 * q + 16, 128 * c : 128 * c + 128]
                out[q // 2, base + (q % 2) * 8 + c] = tile
        block = tn(joined[:, 128 * part : 128 * part + 128], branch[...]).astype(bf)
        for q in range(8):
            for c in range(8):
                tile = block[16 * q : 16 * q + 16, 128 * c : 128 * c + 128]
                out[q % 4, 2 * EARLY + (2 * part + q // 4) * 8 + c] = tile


def late_kernel(info, rows, grad, small, out):
    for q in range(4):
        for half in range(2):
            at = half * (LATE + TEAM) + LATE
            out[q, at : at + TEAM] = small[q, half * TEAM : (half + 1) * TEAM]
    for at in range(0, rows.shape[1], 128):
        block = tn(rows[:, at : at + 128], grad[...]).astype(bf)
        put_rows(out, block, at, MIX_TILES, LATE + TEAM)


def call(kernel, outs, scratch, *args, ties=()):
    ties = jax.tree.leaves(ties)
    specs = [pl.BlockSpec(memory_space=pltpu.SMEM)]
    specs += [pl.BlockSpec(memory_space=pltpu.VMEM)] * (len(args) - 1)
    specs += [pl.BlockSpec(memory_space=pl.ANY)] * len(ties)
    first, last = len(args), len(args) + len(ties)

    def body(*refs):
        kernel(*refs[:first], *refs[last:])

    return pl.pallas_call(
        body,
        out_shape=[jax.ShapeDtypeStruct(s, t) for s, t in outs],
        in_specs=specs,
        out_specs=[pl.BlockSpec(memory_space=pltpu.VMEM)] * len(outs),
        scratch_shapes=[pltpu.VMEM(s, t) for s, t in scratch],
        compiler_params=pltpu.CompilerParams(vmem_limit_bytes=20 * 1024 * 1024),
    )(*args, *ties)


TO_TEAM = [((4, BLOCK, 1024), bf), ((4, BLOCK, 1024), bf)]
CONV_PAD = ((PAD + SEQ, CONV), f32)


def gather_team(x):
    pieces = [x] + [shifted(x, "y", by, 4) for by in (1, 2, 3)]
    return (*pieces, swap(jnp.stack(pieces), "core"))


def sum_team(mine, other):
    pair = mine.astype(f32) + swap(other, "core").astype(f32)
    total = pair[0]
    for by in (1, 2, 3):
        total = total + shifted(pair[by].astype(bf), "y", by, 4).astype(f32)
    return total


def layer_forward(w, x_low, lay, team, before=()):
    info, rowf, colf, trig = lay["info"], lay["rowf"], lay["colf"], lay["trig"]
    x = x_low.astype(f32)
    rows, mixed, cs, qkv, pack = call(
        mix_kernel,
        [((SEQ, 1024), bf), ((SEQ, COLS), f32), ((SEQ, 256), f32), ((SEQ, 256), bf), ((PACKED, 128), bf)],
        [CONV_PAD, ((SEQ, 1024), bf)],
        info, *team, w["gains"], w["mix"], trig, rowf, w["cw"], w["hv"],
    )
    got = after(swap(pack, "zhi"), before)
    keep = jnp.where((jnp.arange(PACKED) < SEQ) | (lay["half"] == 1), 1.0, 0.0).astype(bf)
    got = got * keep[:, None]
    mine, other, joined, ssm, stats = call(
        head_kernel,
        [*TO_TEAM, ((SEQ, 256), bf), ((SEQ, CH), f32), ((SEQ, 128), f32)],
        [CONV_PAD, ((SEQ, CONV), bf), ((128, SEQ), f32), ((128, SEQ), f32)],
        info, mixed, cs, qkv, got, w["out"], rowf, colf, w["cw"], w["hv"],
    )
    resid = x + sum_team(mine, other)
    normed_two, r2 = norm(resid, w["gains"][1])
    team = gather_team(half_first(normed_two.astype(bf)))
    rows_two, gate_up, hidden, mine, other = call(
        ffn_kernel,
        [((SEQ, 1024), bf), ((SEQ, 2 * HID), f32), ((SEQ, HID), bf), *TO_TEAM],
        [],
        info, *team, w["gate_up"], w["down"],
    )
    kept = dict(
        x=x, rows=rows, mixed=mixed, cs=cs, qkv=qkv, got=got, joined=joined, ssm=ssm, stats=stats,
        resid=resid, r2=r2, rows_two=rows_two, gate_up=gate_up, hidden=hidden,
    )
    return (mine, other), kept


def layer_output(parts, kept, lay):
    return (lay["valid"] * (kept["resid"] + sum_team(*parts))).astype(bf)


def layer_backward(w, kept, grad, lay, team, before=(), earlier=((), ())):
    info, rowf, colf, trig = lay["info"], lay["rowf"], lay["colf"], lay["trig"]
    grad_rows, grad_up, mine, other, gain_two = call(
        ffn_back_kernel,
        [((SEQ, 1024), bf), ((SEQ, 2 * HID), bf), *TO_TEAM, ((8, 1024), f32)],
        [],
        info, *team, w["gate_up"], w["down"], kept["gate_up"], kept["rows_two"], w["gains"],
    )
    back = half_first(sum_team(mine, other))
    gx = norm_back(back, kept["resid"], kept["r2"], w["gains"][1])
    grad_resid = grad + gx
    team = gather_team(grad_resid.astype(bf))
    branch_rows, g_act, g_cs, g_qkv, g_z, send, g_skip = call(
        head_back_kernel,
        [((SEQ, 1024), bf), ((SEQ, CONV), f32), ((SEQ, 256), f32), ((SEQ, 256), f32), ((SEQ, CH), f32),
         ((PACKED, 128), bf), ((8, 128), f32)],
        [CONV_PAD, ((SEQ, CONV), bf), ((128, SEQ), f32), ((128, SEQ), f32), ((128, SEQ), f32),
         ((128, SEQ), f32), ((128 + CH, SEQ), f32), ((128, SEQ), f32)],
        info, *team, w["out"], kept["mixed"], kept["cs"], kept["qkv"], kept["got"], kept["ssm"],
        kept["stats"], rowf, colf, w["cw"], w["hv"],
    )
    early = call(
        early_kernel,
        [((4, 2 * EARLY + OUT_TILES, 16, 128), bf)],
        [],
        info, kept["rows_two"], grad_up, kept["hidden"], grad_rows, kept["joined"], branch_rows,
    )[0]
    arrived = to_first(send)
    early_rows = early
    early = lax.psum_scatter(early, "rep", scatter_dimension=0, tiled=False)
    grad_mixed, mine, other, small = call(
        mix_back_kernel,
        [((SEQ, COLS), bf), *TO_TEAM, ((4, 2 * TEAM, 16, 128), bf)],
        [CONV_PAD, CONV_PAD, ((SEQ, 256), f32)],
        info, kept["mixed"], kept["cs"], kept["got"], g_act, g_cs, g_qkv, g_z, g_skip, arrived,
        w["mix"], trig, rowf, w["cw"], w["hv"], kept["rows"], w["gains"], gain_two,
        ties=(early_rows, before, earlier),
    )
    late = call(
        late_kernel,
        [((4, 2 * (LATE + TEAM), 16, 128), bf)],
        [],
        info, kept["rows"], grad_mixed, small,
    )[0]
    back = half_first(sum_team(mine, other))
    late = lax.psum_scatter(late, "rep", scatter_dimension=0, tiled=False)
    r1 = lax.rsqrt(jnp.mean(kept["x"] * kept["x"], axis=-1, keepdims=True) + norm_epsilon)
    gx = norm_back(back, kept["x"], r1, w["gains"][0])
    grads = dict(early=early, late=late)
    return grad_resid + gx, grads


SMALL = 768


def team_columns(w_mix, w_step):
    rows = w_mix.shape[0]
    at = SPACE_CHANNELS + SPACE_CHANNELS
    state = w_mix[:, at : at + 2 * STATE_SIZE]
    at += 2 * STATE_SIZE
    query = w_mix[:, at : at + QUERY_HEADS * HEAD_SIZE].reshape(rows, TEAM, HEAD_SIZE)
    at += QUERY_HEADS * HEAD_SIZE
    key = w_mix[:, at : at + 2 * HEAD_SIZE].reshape(rows, 2, HEAD_SIZE)
    value = w_mix[:, at + 2 * HEAD_SIZE :].reshape(rows, 2, HEAD_SIZE)
    pieces = [
        jnp.broadcast_to(state[:, None], (rows, TEAM, 2 * STATE_SIZE)),
        w_mix[:, SPACE_CHANNELS : 2 * SPACE_CHANNELS].reshape(rows, TEAM, CH),
        w_mix[:, :SPACE_CHANNELS].reshape(rows, TEAM, CH),
        query,
        jnp.repeat(key, TEAM // 2, axis=1),
        jnp.repeat(value, TEAM // 2, axis=1),
        w_step.reshape(rows, TEAM, HEADS),
        jnp.zeros((rows, TEAM, COLS - SMALL_AT), bf),
    ]
    return jnp.moveaxis(jnp.concatenate(pieces, axis=2), 1, 0)


def own_columns(g):
    rows = g.shape[1]

    def joined(at, width):
        return jnp.moveaxis(g[:, :, at : at + width], 0, 1).reshape(rows, TEAM * width)

    def by_group(at):
        part = g[:, :, at : at + HEAD_SIZE].astype(f32).reshape(2, 4, rows, HEAD_SIZE).sum(1)
        return jnp.moveaxis(part, 0, 1).reshape(rows, 2 * HEAD_SIZE).astype(bf)

    state = g[:, :, : 2 * STATE_SIZE].astype(f32).sum(0).astype(bf)
    mix = jnp.concatenate(
        [
            joined(Z_AT, CH),
            joined(X_AT, CH),
            state,
            joined(Q_AT, HEAD_SIZE),
            by_group(Q_AT + HEAD_SIZE),
            by_group(V_AT),
        ],
        axis=1,
    )
    return mix, joined(STEP_AT, HEADS)


def by_layer(blocks):
    own, far, behind, ahead = blocks
    top = lax.axis_index("section") == 0
    return (
        (jnp.where(top, own, behind), jnp.where(top, far, ahead)),
        (jnp.where(top, ahead, own), jnp.where(top, behind, far)),
    )


def in_order(pair):
    first = lax.axis_index("zhi") == 0
    return jnp.where(first, pair[0], pair[1]), jnp.where(first, pair[1], pair[0])


def to_halves(first, second, tiles, top):
    own, away = jnp.where(top, first, second), jnp.where(top, second, first)
    near = swap(away[tiles:], "section").astype(f32)
    cross = lax.ppermute(away[:tiles], RING, [(0, 3), (3, 0), (1, 2), (2, 1)]).astype(f32)
    far = swap(own[:tiles], "zhi").astype(f32)
    total = own[tiles:].astype(f32) + near
    half = total[:tiles] + cross + far
    return half.astype(bf), total[tiles:].astype(bf)


def local(
    layer_input,
    cotangent,
    seq_lengths,
    norm_gains,
    w_mix,
    w_step,
    conv_kernel,
    conv_bias,
    head_params,
    w_out,
    w_gate_up,
    w_down,
):
    section, half = lax.axis_index("section"), lax.axis_index("zhi")
    team = lax.axis_index(("y", "core"))
    top = section == 0
    width = layer_input.shape[-1]

    micro = section

    def of_micro(a):
        return lax.dynamic_index_in_dim(a, micro, 0, False)

    small = jnp.concatenate(
        [norm_gains[0].reshape(-1), conv_kernel[0].reshape(-1), conv_bias[0].reshape(-1)]
    )
    small = jnp.broadcast_to(jnp.pad(small, (0, SMALL - small.shape[0]))[None], (2 * TEAM, SMALL))
    team_axes = ("y", "core")
    x0 = of_micro(layer_input)[0]
    team_x0 = gather_team(x0)
    mix = lax.all_to_all(team_columns(w_mix[0], w_step[0]), team_axes, 0, 0, tiled=True)
    lay = facts(of_micro(seq_lengths)[0], half, team)
    mix = after(mix, lay)
    mix_around = around(mix)
    small, own_heads, cotangent, w_gate_up, w_out = after(
        (small, head_params[0], cotangent, w_gate_up, w_out[0]), mix_around[2], mix_around[3]
    )
    small = lax.all_to_all(small, UNIT_AXES, 0, 0, tiled=True)
    away_small = swap(small, "section")
    away_heads = swap(own_heads, "section")
    up_send = jnp.moveaxis(w_gate_up[0].reshape(BLOCK, 4, TEAM, 128), 2, 0)
    up = lax.all_to_all(up_send.reshape(TEAM, BLOCK, 4 * 128), team_axes, 0, 0, tiled=True)
    w_out, cotangent, up = after((w_out, cotangent, up), mix_around[1])
    out_own = spread_units(w_out.reshape(2, BLOCK, width), lay["info"]).reshape(4 * BLOCK, width)
    out_away = swap(out_own, "section")
    up_around = around(up)
    down_around = around(after(w_down[0], up))
    top_grad = of_micro(cotangent)[0].astype(f32) * lay["valid"]
    team_grad = gather_team(top_grad.astype(bf))
    smalls = []
    for layer in range(2):
        values = jnp.where(top == (layer == 0), small, away_small).astype(f32)
        gains = jnp.moveaxis(values[:, :128].reshape(2 * TEAM, 2, BLOCK), 1, 0).reshape(2, width)
        conv = jnp.moveaxis(values[:, 128:688].reshape(2 * TEAM, KC + 1, 112), 1, 0)
        conv = conv.reshape(KC + 1, XBC)
        conv = jnp.concatenate(
            [conv[:, SPACE_CHANNELS:], lax.dynamic_slice_in_dim(conv, team * CH, CH, 1)], axis=1
        )
        heads = jnp.where(top == (layer == 0), own_heads, away_heads)
        heads = lax.dynamic_slice_in_dim(heads, team * HEADS, HEADS, 1)
        hv = jnp.stack([heads[0], -jnp.exp(heads[1]), heads[2]])
        hv = jnp.pad(hv, ((0, 5), (LANE, 128 - LANE - HEADS)))
        smalls.append(dict(gains=gains, cw=jnp.pad(conv, ((0, 3), (0, 0))), hv=hv))
    team_x0 = after(team_x0, smalls)
    mix_layers = by_layer(mix_around)
    up_layers = by_layer(up_around)
    down_layers = by_layer(down_around)
    weights = []
    for layer in range(2):
        own_layer = top if layer == 0 else jnp.logical_not(top)
        weights.append(
            dict(
                smalls[layer],
                mix=jnp.concatenate([m.reshape(SEQ, COLS) for m in mix_layers[layer]]),
                out=jnp.where(own_layer, out_own, out_away),
                gate_up=jnp.concatenate([u.reshape(SEQ, 2 * HID) for u in up_layers[layer]]),
                down=jnp.concatenate(in_order(down_layers[layer])),
            )
        )
    parts0, kept0 = layer_forward(weights[0], x0, lay, team_x0, (up_around, down_around, team_grad))
    act0 = layer_output(parts0, kept0, lay)
    parts1, kept1 = layer_forward(weights[1], act0, lay, gather_team(act0))
    act1 = layer_output(parts1, kept1, lay)
    grad1, grads1 = layer_backward(weights[1], kept1, top_grad, lay, team_grad, act1)
    low_grad = grad1.astype(bf).astype(f32) * lay["valid"]
    grad0, grads0 = layer_backward(
        weights[0], kept0, low_grad, lay, gather_team(low_grad.astype(bf)), (),
        (grads1["early"], grads1["late"]),
    )

    def placed(first, second):
        other = swap(jnp.where(top, second, first).astype(bf), "section")
        own = jnp.where(top, first, second)
        other = other.astype(own.dtype)
        return jnp.where(top, jnp.stack([own, other]), jnp.stack([other, own]))

    activations = placed(act0, act1)
    input_grads = placed(grad0, grad1)

    early_half, early_out = to_halves(grads0["early"], grads1["early"], EARLY, top)
    early_out = (early_out.astype(f32) + swap(early_out, "zhi").astype(f32)).astype(bf)
    late, _ = to_halves(grads0["late"], grads1["late"], LATE + TEAM, top)
    early = call(
        send_early_kernel,
        [((TEAM, UP_TILES + 16, 16, 128), bf)],
        [],
        lay["info"], early_half, early_out.reshape(4, 8, 16, 128), ties=late,
    )[0]
    early = lax.all_to_all(early, ("y", "core"), 0, 0, tiled=True)
    early = call(
        got_early_kernel,
        [((TEAM * UP_TILES + DOWN_TILES + 16, 16, 128), bf)],
        [],
        lay["info"], early, early_half,
    )[0]
    early = gather_ring(early, "rep")
    count = TEAM * UP_TILES
    up = early[:, :count].reshape(4, TEAM, UP_TILES, 16, 128)
    up = jnp.transpose(up, (0, 3, 2, 1, 4)).reshape(BLOCK, 2 * FF)
    down = early[:, count : count + DOWN_TILES].reshape(4, 2, 8, 16, 128)
    down = jnp.transpose(down, (0, 1, 3, 2, 4)).reshape(128, width)
    out = early[:, count + DOWN_TILES :].reshape(4, 2, 8, 16, 128)
    out = jnp.transpose(out, (1, 0, 3, 2, 4)).reshape(128, width)

    late = jnp.concatenate(
        [late[:LATE].reshape(TEAM, MIX_TILES, 16, 128), late[LATE:].reshape(TEAM, 1, 16, 128)], axis=1
    )
    late = lax.all_to_all(late, ("y", "core"), 0, 0, tiled=True)
    mix, step = own_columns(jnp.moveaxis(late[:, :MIX_TILES], 1, 2).reshape(TEAM, 16, COLS))
    values = jnp.moveaxis(late[:, MIX_TILES], 0, 1).reshape(16, TEAM * 128)
    step = jnp.pad(step, ((0, 0), (0, 128 - MIXER_HEADS)))
    mix = gather_ring(jnp.concatenate([mix, step, values], axis=1), "rep")
    values = mix[:, :, w_mix.shape[2] + 128 :].reshape(4, 16, TEAM, 128).astype(f32)
    gains = values[0, :2, :, :BLOCK].sum(1)
    heads = values[0, 2:5, :, LANE : LANE + HEADS].reshape(3, MIXER_HEADS)
    state = values[1].sum(1).reshape(16, 128)
    state = jnp.concatenate([state[: KC + 1], state[KC + 1 : 2 * (KC + 1)]], axis=1)
    inner = jnp.concatenate(
        [values[2, : KC + 1], values[2, KC + 1 : 2 * (KC + 1), :, : CH - 128]], axis=2
    )
    conv = jnp.concatenate([inner.reshape(KC + 1, SPACE_CHANNELS), state], axis=1)
    owner = lax.axis_index(UNIT_AXES)
    conv = lax.dynamic_slice_in_dim(conv, owner * 112, 112, 1)
    mix = mix.reshape(BLOCK, -1)
    return (
        activations[None, :, None],
        input_grads[None, :, None],
        gains[None],
        mix[:, : w_mix.shape[2]].astype(f32)[None],
        mix[:, w_mix.shape[2] : w_mix.shape[2] + MIXER_HEADS].astype(f32)[None],
        conv[:KC][None],
        conv[KC][None],
        heads[None],
        out.astype(f32)[None],
        up.astype(f32)[None],
        down.astype(f32)[None],
    )


def solution(mesh):
    devices = mesh.devices.reshape(2, 2, 4, 2, 4)
    fine = Mesh(devices, ("section", "zhi", "y", "core", "rep"))
    fsdp = ("zhi", "y", "core")
    in_specs = (
        P(None, "rep", fsdp, None),
        P(None, "rep", fsdp, None),
        P(None, "rep", None),
        P("section", None, fsdp),
        P("section", fsdp, None),
        P("section", fsdp, None),
        P("section", None, fsdp),
        P("section", fsdp),
        P("section", None, None),
        P("section", fsdp, None),
        P("section", fsdp, None),
        P("section", fsdp, None),
    )
    out_specs = (
        P("section", None, "rep", fsdp, None),
        P("section", None, "rep", fsdp, None),
        P("section", None, fsdp),
        P("section", fsdp, None),
        P("section", fsdp, None),
        P("section", None, fsdp),
        P("section", fsdp),
        P("section", None, None),
        P("section", fsdp, None),
        P("section", fsdp, None),
        P("section", fsdp, None),
    )
    return jax.shard_map(local, mesh=fine, in_specs=in_specs, out_specs=out_specs, check_vma=False)
```

time: 1980 us -> 608 us (0.31)
  waiting for transfers between devices: 701 us -> 203 us
  blocking collectives: 325 us -> 0 us
  matrix products: 266 us -> 0 us
  other arithmetic: 280 us -> 44.6 us
  local copies, waits for them, and re-layouts: 281 us -> 85.6 us
  Pallas kernels: 0 us -> 87.5 us
  starting transfers between devices: 78.4 us -> 158 us
    reduce_scatter x4, waiting for transfers between devices: 338 us -> 6.38 us  [the longest x2 6.36 us: layer_backward(): late = lax.psum_scatter(late, 'rep', scatter_dimension=0, tiled=False)]
    dot_general x98 -> x0, matrix products: 266 us -> none  [the longest x15 50.1 us: bf_dot(): return jnp.dot(left, right, preferred_element_type=jnp.float32)]
    all_gather x10 -> x0, waiting for transfers between devices: 235 us -> none  [the longest x1 69.9 us: local(): lax.all_gather(w_gate_up[0], 'fsdp', axis=0, tiled=True)]
    all_gather x8 -> x0, blocking collectives: 218 us -> none  [the longest x3 86 us: carried_in(): lax.all_gather(part.astype(kind), axis)]
    ppermute x10 -> x102, waiting for transfers between devices: 19.5 us -> 183 us  [the longest x54 109 us: shifted(): lax.ppermute(x, axis, [(i, (i + by) % devices) for i in range(devices)])]
    ppermute x10 -> x102, starting transfers between devices: 27.3 us -> 129 us  [the longest x54 54.4 us: shifted(): lax.ppermute(x, axis, [(i, (i + by) % devices) for i in range(devices)])]
    unnamed x2 -> x0, blocking collectives: 94 us -> none
    pallas_call x0 -> x20, Pallas kernels: none -> 87.5 us  [call(): pl.pallas_call(body, out_shape=[jax.ShapeDtypeStruct(s, t) for s, t in ou...]
  transfers between devices with their start and end apart: 33 -> 111, of which waited for: 23 -> 70; matrix products, arithmetic and copies ran while one was open for 21% -> 10% of each run, Pallas kernels for 0% -> 8%
where the time goes in v1:
time: 608 us; the launch traced here: 597 us
  waiting for transfers between devices  203 us (33%)
  starting transfers between devices  158 us (26%)
  Pallas kernels  87.5 us (14%)
  local copies, waits for them, and re-layouts  85.6 us (14%)
  other arithmetic  44.6 us (7%)
  between operations  17.6 us (3%)
    ppermute x54, waiting for transfers between devices, shifted(): lax.ppermute(x, axis, [(i, (i + by) % devices) for i in range(devices)])  109 us
    pallas_call x20, Pallas kernels, call(): pl.pallas_call(body, out_shape=[jax.ShapeDtypeStruct(s, t) for s, t in ou...  87.5 us
    ppermute x54, starting transfers between devices, shifted(): lax.ppermute(x, axis, [(i, (i + by) % devices) for i in range(devices)])  54.4 us
    unnamed x414, local copies, waits for them, and re-layouts  49.2 us
    ppermute x28, starting transfers between devices, swap(): return lax.ppermute(x, axis, [(0, 1), (1, 0)])  38.3 us
    ppermute x28, waiting for transfers between devices, swap(): return lax.ppermute(x, axis, [(0, 1), (1, 0)])  29.6 us
    ppermute x4, starting transfers between devices, spread_units(): lax.ppermute(piece, UNIT_AXES, [(e[0], e[1]) for e in route])  14.3 us
    ppermute x3, waiting for transfers between devices, around(): lax.ppermute(behind[:half], RING, FORWARD)  13.1 us
  transfers between devices with their start and end apart: 111, of which 70 were waited for; matrix products, arithmetic and copies ran while one was open for 10% of the time, Pallas kernels for 8%

profile of v1, /device:TPU:1, one launch (start us, length us, event | category | flops | bytes accessed | tf_op | source)
XLA Modules:
  0.0 596.8 jit_solution(6296766256936347477)
XLA Ops:
  14.5 6.0 %all-to-all-start = ((bf16[8,64,896]{2,1,0:T(8,128)(2,1)}), bf16[8,64,896]{2,1,0:T(8,128)(2,1)S(1)}, u32[]{:S(2)}, u32[]{:S(2)}) async-start(bf16[8,64,896]{2,1,0:T(8,128)(2,1)} %bitcast.14), calls=%async_computation | async-start | bytes 1835008 | tf_op jit(solution)/shard_map/all_to_all | solution.py:984
  28.2 5.9 all-to-all-done
  51.3 6.5 %collective-permute-done.4 = bf16[8,64,896]{2,1,0:T(8,128)(2,1)} collective-permute-done((bf16[8,64,896]{2,1,0:T(8,128)(2,1)S(1)}, bf16[8,64,896]{2,1,0:T(8,128)(2,1)}, u32[]{:S(2)}, u32[]{:S(2)}) %collective-permute-start.4) | collective-permute-done | bytes 917536 | tf_op jit(solution)/shard_map/ppermute | solution.py:77
  59.6 6.3 %all-to-all-start.1 = ((bf16[16,2,384]{2,1,0:T(2,128)(2,1)}), bf16[16,2,384]{2,1,0:T(2,128)(2,1)S(1)}, u32[]{:S(2)}, u32[]{:S(2)}) async-start(bf16[16,2,384]{2,1,0:T(2,128)(2,1)} %reshape.810), calls=%async_computation.1 | async-start | bytes 49152 | tf_op jit(solution)/shard_map/all_to_all | solution.py:991
  75.0 5.8 all-to-all-start.2
  94.8 4.8 collective-permute-start.23
  110.3 3.9 collective-permute-start.26
  125.2 4.1 collective-permute-done.20.refs_3_
  136.4 8.1 %collective-permute-done.16 = bf16[64,1024]{1,0:T(8,128)(2,1)S(1)} collective-permute-done((bf16[64,1024]{1,0:T(8,128)(2,1)S(1)}, bf16[64,1024]{1,0:T(8,128)(2,1)S(1)}, u32[]{:S(2)}, u32[]{:S(2)}) %collective-permute-start.16) | collective-permute-done | bytes 131104 | tf_op jit(solution)/shard_map/ppermute | solution.py:80
  151.7 5.0 collective-permute-done.12
  158.6 5.9 shard_map.215
  204.2 4.8 collective-permute-done.39
  216.1 6.2 %collective-permute-done.40.refs_2_ = bf16[64,1024]{1,0:T(8,128)(2,1)S(1)} collective-permute-done((bf16[64,1024]{1,0:T(8,128)(2,1)S(1)}, bf16[64,1024]{1,0:T(8,128)(2,1)S(1)}, u32[]{:S(2)}, u32[]{:S(2)}) %collective-permute-start.40) | collective-permute-done | bytes 131104 | tf_op jit(solution)/shard_map/ppermute | solution.py:56
  225.7 3.9 shard_map.217
  233.6 4.8 collective-permute-done.44
  238.5 5.9 shard_map.218
  266.6 6.0 %collective-permute-done.49.refs_2_ = bf16[64,1024]{1,0:T(8,128)(2,1)S(1)} collective-permute-done((bf16[64,1024]{1,0:T(8,128)(2,1)S(1)}, bf16[64,1024]{1,0:T(8,128)(2,1)S(1)}, u32[]{:S(2)}, u32[]{:S(2)}) %collective-permute-start.49) | collective-permute-done | bytes 131104 | tf_op jit(solution)/shard_map/ppermute | solution.py:56
  301.1 6.1 %collective-permute-done.62.refs_2_ = bf16[64,1024]{1,0:T(8,128)(2,1)S(1)} collective-permute-done((bf16[64,1024]{1,0:T(8,128)(2,1)S(1)}, bf16[64,1024]{1,0:T(8,128)(2,1)S(1)}, u32[]{:S(2)}, u32[]{:S(2)}) %collective-permute-start.62) | collective-permute-done | bytes 131104 | tf_op jit(solution)/shard_map/ppermute | solution.py:56
  310.8 14.1 %shard_map.221 = (bf16[512,1024]{1,0:T(8,128)(2,1)S(1)}, f32[512,448]{1,0:T(8,128)S(1)}, f32[512,256]{1,0:T(8,128)S(1)}, f32[512,256]{1,0:T(8,128)S(1)}, f32[512...) custom-call(s32[30]{0:T(128)S(1)} %copy-done.107, ...), custom_call_target="tpu_custom_call" | custom-call | tf_op jit(solution)/shard_map/pallas_call | solution.py:762
  355.2 7.3 %shard_map.223 = (bf16[512,896]{1,0:T(8,128)(2,1)S(1)}, bf16[4,64,1024]{2,1,0:T(8,128)(2,1)S(1)}, bf16[4,64,1024]{2,1,0:T(8,128)(2,1)S(1)}, bf16[4,16,16,128]{3,2,1,0:T(8,128)(2,1)S(1)}) custom-call(s32[30]{0:T(128)S(1)} %copy-done.108, f32[512,896]{1,0:T(8,128)S(1)} %copy-done.7, f32[512,256]{1,0:T(8,128)S(1)} %copy-done.13, ...), custom_call_target="tpu_custom_call" | custom-call | tf_op jit(solution)/shard_map/pallas_call | solution.py:762
  408.8 3.8 collective-permute-done.76
  416.6 6.3 %collective-permute-done.79.refs_2_ = bf16[64,1024]{1,0:T(8,128)(2,1)S(1)} collective-permute-done((bf16[64,1024]{1,0:T(8,128)(2,1)S(1)}, bf16[64,1024]{1,0:T(8,128)(2,1)S(1)}, u32[]{:S(2)}, u32[]{:S(2)}) %collective-permute-start.79) | collective-permute-done | bytes 131104 | tf_op jit(solution)/shard_map/ppermute | solution.py:56
  426.2 14.1 %shard_map.225 = (bf16[512,1024]{1,0:T(8,128)(2,1)S(1)}, f32[512,448]{1,0:T(8,128)S(1)}, f32[512,256]{1,0:T(8,128)S(1)}, f32[512,256]{1,0:T(8,128)S(1)}, f32[512...) custom-call(s32[30]{0:T(128)S(1)} %copy-done.110, ...), custom_call_target="tpu_custom_call" | custom-call | tf_op jit(solution)/shard_map/pallas_call | solution.py:762
  449.7 8.2 %collective-permute-done.83.refs_9_ = bf16[768,128]{1,0:T(8,128)(2,1)S(1)} collective-permute-done((bf16[768,128]{1,0:T(8,128)(2,1)}, bf16[768,128]{1,0:T(8,128)(2,1)S(1)}, u32[]{:S(2)}, u32[]{:S(2)}) %collective-permute-start.83) | collective-permute-done | bytes 196640 | tf_op jit(solution)/shard_map/ppermute | solution.py:257
  473.2 7.3 %shard_map.228 = (bf16[512,896]{1,0:T(8,128)(2,1)S(1)}, bf16[4,64,1024]{2,1,0:T(8,128)(2,1)S(1)}, bf16[4,64,1024]{2,1,0:T(8,128)(2,1)S(1)}, bf16[4,16,16,128]{3,2,1,0:T(8,128)(2,1)S(1)}) custom-call(s32[30]{0:T(128)S(1)} %copy-done.111, f32[512,896]{1,0:T(8,128)S(1)} %copy-done.2, f32[512,256]{1,0:T(8,128)S(1)} %get-tuple-element.102.refs_2_.refs_8_, ...), custom_call_target="tpu_custom_call" | custom-call | tf_op jit(solution)/shard_map/pallas_call | solution.py:762
  508.7 6.4 %reduce-scatter.9.cloned.1.call-done = bf16[1,128,16,128]{3,2,1,0:T(8,128)(2,1)} async-done(((bf16[4,128,16,128]{3,2,1,0:T(8,128)(2,1)}), bf16[1,128,16,128]{3,2,1,0:T(8,128)(2,1)}) %reduce-scatter.9.cloned.1.call-update) | async-done | bytes 524304 | tf_op jit(solution)/shard_map/reduce_scatter | solution.py:872
  528.0 4.6 collective-permute-done.90
  533.5 5.3 all-to-all-start.3
  538.9 4.0 collective-permute-done.96
  550.2 5.3 all-to-all-start.4
  560.9 5.6 all-to-all-done.4.refs_1_
  577.7 7.2 %collective-permute-done.99 = bf16[64,16,128]{2,1,0:T(8,128)(2,1)S(1)} collective-permute-done((bf16[64,16,128]{2,1,0:T(8,128)(2,1)S(1)}, bf16[64,16,128]{2,1,0:T(8,128)(2,1)S(1)}, u32[]{:S(2)}, u32[]{:S(2)}) %collective-permute-start.99) | collective-permute-done | bytes 262176 | tf_op jit(solution)/shard_map/ppermute | solution.py:56
  (887 shorter events, 379.7 us)
Async XLA Ops:
  14.5 19.7 %all-to-all-start = ((bf16[8,64,896]{2,1,0:T(8,128)(2,1)}), bf16[8,64,896]{2,1,0:T(8,128)(2,1)S(1)}, u32[]{:S(2)}, u32[]{:S(2)}) async-start(bf16[8,64,896]{2,1,0:T(8,128)(2,1)} %bitcast.14), calls=%async_computation | async-start | bytes 1835008 | tf_op jit(solution)/shard_map/all_to_all | solution.py:984
  34.1 23.7 %collective-permute-start.4 = (bf16[8,64,896]{2,1,0:T(8,128)(2,1)S(1)}, bf16[8,64,896]{2,1,0:T(8,128)(2,1)}, u32[]{:S(2)}, u32[]{:S(2)}) collective-permute-start(bf16[8,64,896]{2,1,0:T(8,128)(2,1)S(1)} %all-to-all-done), channel_id=1, source_target_pairs={{0,64},{64,32},{32,96},{96,0},{1,65},{65,33},{33,97},{97,1},{2,66}... | collective-permute-start | bytes 2752520 | tf_op jit(solution)/shard_map/ppermute | solution.py:77
  35.8 22.1 %collective-permute-start.5 = (bf16[8,64,896]{2,1,0:T(8,128)(2,1)S(1)}, bf16[8,64,896]{2,1,0:T(8,128)(2,1)}, u32[]{:S(2)}, u32[]{:S(2)}) collective-permute-start(bf16[8,64,896]{2,1,0:T(8,128)(2,1)S(1)} %all-to-all-done), channel_id=1, source_target_pairs={{64,0},{32,64},{96,32},{0,96},{65,1},{33,65},{97,33},{1,97},{66,2}... | collective-permute-start | bytes 2752520 | tf_op jit(solution)/shard_map/ppermute | solution.py:78
  49.1 38.5 %collective-permute-start.3 = (bf16[4,64,1024]{2,1,0:T(8,128)(2,1)}, bf16[4,64,1024]{2,1,0:T(8,128)(2,1)S(1)}, u32[]{:S(2)}, u32[]{:S(2)}) collective-permute-start(bf16[4,64,1024]{2,1,0:T(8,128)(2,1)} %pad_maximum_fusion.6), channel_id=1, source_target_pairs={{0,4},{4,0},{1,5},{5,1},{2,6},{6,2},{3,7},{7,3},{8,12},{12,8},{9,1... | collective-permute-start | bytes 1572872 | tf_op jit(solution)/shard_map/ppermute | solution.py:60
  59.6 15.4 %all-to-all-start.1 = ((bf16[16,2,384]{2,1,0:T(2,128)(2,1)}), bf16[16,2,384]{2,1,0:T(2,128)(2,1)S(1)}, u32[]{:S(2)}, u32[]{:S(2)}) async-start(bf16[16,2,384]{2,1,0:T(2,128)(2,1)} %reshape.810), calls=%async_computation.1 | async-start | bytes 49152 | tf_op jit(solution)/shard_map/all_to_all | solution.py:991
  68.3 19.3 %collective-permute-start.8 = (bf16[4,64,896]{2,1,0:T(8,128)(2,1)}, bf16[4,64,896]{2,1,0:T(8,128)(2,1)}, u32[]{:S(2)}, u32[]{:S(2)}) collective-permute-start(bf16[4,64,896]{2,1,0:T(8,128)(2,1)} %slice.499), channel_id=1, source_target_pairs={{0,64},{64,32},{32,96},{96,0},{1,65},{65,33},{33,97},{97,1},{2,66}... | collective-permute-start | bytes 1376264 | tf_op jit(solution)/shard_map/ppermute | solution.py:80
  71.0 18.7 %collective-permute-start.9 = (bf16[4,64,896]{2,1,0:T(8,128)(2,1)}, bf16[4,64,896]{2,1,0:T(8,128)(2,1)}, u32[]{:S(2)}, u32[]{:S(2)}) collective-permute-start(bf16[4,64,896]{2,1,0:T(8,128)(2,1)} %slice.500), channel_id=1, source_target_pairs={{64,0},{32,64},{96,32},{0,96},{65,1},{33,65},{97,33},{1,97},{66,2}... | collective-permute-start | bytes 1376264 | tf_op jit(solution)/shard_map/ppermute | solution.py:81
  75.0 16.5 %all-to-all-start.2 = ((bf16[8,64,512]{2,1,0:T(8,128)(2,1)}), bf16[8,64,512]{2,1,0:T(8,128)(2,1)S(1)}, u32[]{:S(2)}, u32[]{:S(2)}) async-start(bf16[8,64,512]{2,1,0:T(8,128)(2,1)} %reshape.734), calls=%async_computation.2 | async-start | bytes 1048576 | tf_op jit(solution)/shard_map/all_to_all | solution.py:995
  80.8 377.9 %reduce-scatter.5.cloned.1.call-start = ((), (), s32[]{:S(2)}) async-start(), calls=%async_computation.9 | async-start | bytes 2621440 | tf_op jit(solution)/shard_map/reduce_scatter | solution.py:856
  91.5 32.5 %collective-permute-start.15 = (bf16[128,1024]{1,0:T(8,128)(2,1)}, bf16[128,1024]{1,0:T(8,128)(2,1)S(1)}, u32[]{:S(2)}, u32[]{:S(2)}) collective-permute-start(bf16[128,1024]{1,0:T(8,128)(2,1)} %bitcast.36), channel_id=1, source_target_pairs={{0,64},{64,32},{32,96},{96,0},{1,65},{65,33},{33,97},{97,1},{2,66}... | collective-permute-start | bytes 786440 | tf_op jit(solution)/shard_map/ppermute | solution.py:77
  91.5 37.8 %collective-permute-start.17 = (bf16[128,1024]{1,0:T(8,128)(2,1)}, bf16[128,1024]{1,0:T(8,128)(2,1)S(1)}, u32[]{:S(2)}, u32[]{:S(2)}) collective-permute-start(bf16[128,1024]{1,0:T(8,128)(2,1)} %bitcast.36), channel_id=1, source_target_pairs={{64,0},{32,64},{96,32},{0,96},{65,1},{33,65},{97,33},{1,97},{66,2}... | collective-permute-start | bytes 786440 | tf_op jit(solution)/shard_map/ppermute | solution.py:78
  94.8 13.6 %collective-permute-start.23 = (bf16[64,1024]{1,0:T(8,128)(2,1)S(1)}, bf16[64,1024]{1,0:T(8,128)(2,1)S(1)}, u32[]{:S(2)}, u32[]{:S(2)}) collective-permute-start(bf16[64,1024]{1,0:T(8,128)(2,1)S(1)} %get-tuple-element.113), channel_id=1, source_target_pairs={{0,0},{4,8},{8,16},{12,24},{16,32},{20,36},{24,4},{28,40},{32,44},... | collective-permute-start | bytes 393224 | tf_op jit(solution)/shard_map/ppermute | solution.py:179
  104.3 19.7 %collective-permute-start.19 = (bf16[64,1024]{1,0:T(8,128)(2,1)S(1)}, bf16[64,1024]{1,0:T(8,128)(2,1)S(1)}, u32[]{:S(2)}, u32[]{:S(2)}) collective-permute-start(bf16[64,1024]{1,0:T(8,128)(2,1)S(1)} %fusion.5.refs_1_), channel_id=1, source_target_pairs={{0,8},{8,16},{16,24},{24,0},{1,9},{9,17},{17,25},{25,1},{2,10},{10... | collective-permute-start | bytes 393224 | tf_op jit(solution)/shard_map/ppermute | solution.py:56
  120.1 27.8 %collective-permute-start.11 = (bf16[8,64,512]{2,1,0:T(8,128)(2,1)S(1)}, bf16[8,64,512]{2,1,0:T(8,128)(2,1)S(1)}, u32[]{:S(2)}, u32[]{:S(2)}) collective-permute-start(bf16[8,64,512]{2,1,0:T(8,128)(2,1)S(1)} %copy-done.149), channel_id=1, source_target_pairs={{0,64},{64,32},{32,96},{96,0},{1,65},{65,33},{33,97},{97,1},{2,66}... | collective-permute-start | bytes 1572872 | tf_op jit(solution)/shard_map/ppermute | solution.py:77
  120.1 27.9 %collective-permute-start.13 = (bf16[8,64,512]{2,1,0:T(8,128)(2,1)S(1)}, bf16[8,64,512]{2,1,0:T(8,128)(2,1)S(1)}, u32[]{:S(2)}, u32[]{:S(2)}) collective-permute-start(bf16[8,64,512]{2,1,0:T(8,128)(2,1)S(1)} %copy-done.149), channel_id=1, source_target_pairs={{64,0},{32,64},{96,32},{0,96},{65,1},{33,65},{97,33},{1,97},{66,2}... | collective-permute-start | bytes 1572872 | tf_op jit(solution)/shard_map/ppermute | solution.py:78
  124.2 26.6 %collective-permute-start.27 = (bf16[256,1024]{1,0:T(8,128)(2,1)S(1)}, bf16[256,1024]{1,0:T(8,128)(2,1)S(1)}, u32[]{:S(2)}, u32[]{:S(2)}) collective-permute-start(bf16[256,1024]{1,0:T(8,128)(2,1)S(1)} %bitcast.374), channel_id=1, source_target_pairs={{0,64},{64,0},{1,65},{65,1},{2,66},{66,2},{3,67},{67,3},{4,68},{68... | collective-permute-start | bytes 1572872 | tf_op jit(solution)/shard_map/ppermute | solution.py:60
  129.4 15.1 %collective-permute-start.16 = (bf16[64,1024]{1,0:T(8,128)(2,1)S(1)}, bf16[64,1024]{1,0:T(8,128)(2,1)S(1)}, u32[]{:S(2)}, u32[]{:S(2)}) collective-permute-start(bf16[64,1024]{1,0:T(8,128)(2,1)S(1)} %slice.503), channel_id=1, source_target_pairs={{0,64},{64,32},{32,96},{96,0},{1,65},{65,33},{33,97},{97,1},{2,66}... | collective-permute-start | bytes 393224 | tf_op jit(solution)/shard_map/ppermute | solution.py:80
  133.9 13.9 %collective-permute-start.18 = (bf16[64,1024]{1,0:T(8,128)(2,1)S(1)}, bf16[64,1024]{1,0:T(8,128)(2,1)S(1)}, u32[]{:S(2)}, u32[]{:S(2)}) collective-permute-start(bf16[64,1024]{1,0:T(8,128)(2,1)S(1)} %slice.504), channel_id=1, source_target_pairs={{64,0},{32,64},{96,32},{0,96},{65,1},{33,65},{97,33},{1,97},{66,2}... | collective-permute-start | bytes 393224 | tf_op jit(solution)/shard_map/ppermute | solution.py:81
  144.4 12.4 %collective-permute-start.10 = (bf16[768,128]{1,0:T(8,128)(2,1)S(1)}, bf16[768,128]{1,0:T(8,128)(2,1)S(1)}, u32[]{:S(2)}, u32[]{:S(2)}) collective-permute-start(bf16[768,128]{1,0:T(8,128)(2,1)S(1)} %get-tuple-element.104), channel_id=1, source_target_pairs={{0,32},{32,0},{1,33},{33,1},{2,34},{34,2},{3,35},{35,3},{4,36},{36... | collective-permute-start | bytes 589832 | tf_op jit(solution)/shard_map/ppermute | solution.py:60
  332.2 126.4 %reduce-scatter.7.cloned.1.call-start = ((), (), s32[]{:S(2)}) async-start(), calls=%async_computation.10 | async-start | bytes 2621440 | tf_op jit(solution)/shard_map/reduce_scatter | solution.py:872
  367.5 12.1 %collective-permute-start.70 = (bf16[64,1024]{1,0:T(8,128)(2,1)}, bf16[64,1024]{1,0:T(8,128)(2,1)}, u32[]{:S(2)}, u32[]{:S(2)}) collective-permute-start(bf16[64,1024]{1,0:T(8,128)(2,1)} %get-tuple-element.305), channel_id=1, source_target_pairs={{0,24},{8,0},{16,8},{24,16},{1,25},{9,1},{17,9},{25,17},{2,26},{10... | collective-permute-start | bytes 393224 | tf_op jit(solution)/shard_map/ppermute | solution.py:56
  379.5 126.7 %reduce-scatter.11.cloned.1.call-start = ((), (), s32[]{:S(2)}) async-start(), calls=%async_computation.12 | async-start | bytes 2621440 | tf_op jit(solution)/shard_map/reduce_scatter | solution.py:856
  448.2 66.9 %reduce-scatter.9.cloned.1.call-start = ((), (), s32[]{:S(2)}) async-start(), calls=%async_computation.11 | async-start | bytes 2621440 | tf_op jit(solution)/shard_map/reduce_scatter | solution.py:872
  507.4 16.7 %collective-permute-start.95 = (bf16[80,16,128]{2,1,0:T(8,128)(2,1)S(1)}, bf16[80,16,128]{2,1,0:T(8,128)(2,1)S(1)}, u32[]{:S(2)}, u32[]{:S(2)}) collective-permute-start(bf16[80,16,128]{2,1,0:T(8,128)(2,1)S(1)} %slice.579), channel_id=1, source_target_pairs={{0,64},{64,0},{1,65},{65,1},{2,66},{66,2},{3,67},{67,3},{4,68},{68... | collective-permute-start | bytes 983048 | tf_op jit(solution)/shard_map/ppermute | solution.py:60
  519.2 13.4 %collective-permute-start.90 = (bf16[64,16,128]{2,1,0:T(8,128)(2,1)S(1)}, bf16[64,16,128]{2,1,0:T(8,128)(2,1)S(1)}, u32[]{:S(2)}, u32[]{:S(2)}) collective-permute-start(bf16[64,16,128]{2,1,0:T(8,128)(2,1)S(1)} %get-tuple-element.297), channel_id=1, source_target_pairs={{0,96},{96,0},{32,64},{64,32},{1,97},{97,1},{33,65},{65,33},{2,98}... | collective-permute-start | bytes 786440 | tf_op jit(solution)/shard_map/ppermute | solution.py:946
  520.1 12.5 %collective-permute-start.89 = (bf16[64,16,128]{2,1,0:T(8,128)(2,1)S(1)}, bf16[64,16,128]{2,1,0:T(8,128)(2,1)S(1)}, u32[]{:S(2)}, u32[]{:S(2)}) collective-permute-start(bf16[64,16,128]{2,1,0:T(8,128)(2,1)S(1)} %get-tuple-element.296), channel_id=1, source_target_pairs={{0,64},{64,0},{1,65},{65,1},{2,66},{66,2},{3,67},{67,3},{4,68},{68... | collective-permute-start | bytes 786440 | tf_op jit(solution)/shard_map/ppermute | solution.py:60
  521.0 17.9 %collective-permute-start.97 = (bf16[48,16,128]{2,1,0:T(8,128)(2,1)S(1)}, bf16[48,16,128]{2,1,0:T(8,128)(2,1)S(1)}, u32[]{:S(2)}, u32[]{:S(2)}) collective-permute-start(bf16[48,16,128]{2,1,0:T(8,128)(2,1)S(1)} %slice.582), channel_id=1, source_target_pairs={{0,32},{32,0},{1,33},{33,1},{2,34},{34,2},{3,35},{35,3},{4,36},{36... | collective-permute-start | bytes 589832 | tf_op jit(solution)/shard_map/ppermute | solution.py:60
  524.1 18.8 %collective-permute-start.96 = (bf16[48,16,128]{2,1,0:T(8,128)(2,1)S(1)}, bf16[48,16,128]{2,1,0:T(8,128)(2,1)S(1)}, u32[]{:S(2)}, u32[]{:S(2)}) collective-permute-start(bf16[48,16,128]{2,1,0:T(8,128)(2,1)S(1)} %slice.581), channel_id=1, source_target_pairs={{0,96},{96,0},{32,64},{64,32},{1,97},{97,1},{33,65},{65,33},{2,98}... | collective-permute-start | bytes 589832 | tf_op jit(solution)/shard_map/ppermute | solution.py:946
  525.3 23.5 %collective-permute-start.98 = (bf16[32,16,128]{2,1,0:T(8,128)(2,1)S(1)}, bf16[32,16,128]{2,1,0:T(8,128)(2,1)S(1)}, u32[]{:S(2)}, u32[]{:S(2)}) collective-permute-start(bf16[32,16,128]{2,1,0:T(8,128)(2,1)S(1)} %slice.721), channel_id=1, source_target_pairs={{0,32},{32,0},{1,33},{33,1},{2,34},{34,2},{3,35},{35,3},{4,36},{36... | collective-permute-start | bytes 393224 | tf_op jit(solution)/shard_map/ppermute | solution.py:60
  533.5 11.8 %all-to-all-start.3 = ((bf16[8,8,16,128]{3,2,1,0:T(8,128)(2,1)}), bf16[8,8,16,128]{3,2,1,0:T(8,128)(2,1)S(1)}, u32[]{:S(2)}, u32[]{:S(2)}) async-start(bf16[8,8,16,128]{3,2,1,0:T(8,128)(2,1)} %pad_maximum_fusion.16), calls=%async_computation.6 | async-start | bytes 524288 | tf_op jit(solution)/shard_map/all_to_all | solution.py:1081
  550.2 16.2 %all-to-all-start.4 = ((bf16[8,20,16,128]{3,2,1,0:T(8,128)(2,1)}), bf16[8,20,16,128]{3,2,1,0:T(8,128)(2,1)S(1)}, u32[]{:S(2)}, u32[]{:S(2)}) async-start(bf16[8,20,16,128]{3,2,1,0:T(8,128)(2,1)} %shard_map.230), calls=%async_computation.8 | async-start | bytes 1310720 | tf_op jit(solution)/shard_map/all_to_all | solution.py:1062
  570.2 14.7 %collective-permute-start.99 = (bf16[64,16,128]{2,1,0:T(8,128)(2,1)S(1)}, bf16[64,16,128]{2,1,0:T(8,128)(2,1)S(1)}, u32[]{:S(2)}, u32[]{:S(2)}) collective-permute-start(bf16[64,16,128]{2,1,0:T(8,128)(2,1)S(1)} %shard_map.231), channel_id=1, source_target_pairs={{0,1},{1,2},{2,3},{3,0},{4,5},{5,6},{6,7},{7,4},{8,9},{9,10},{10,1... | collective-permute-start | bytes 786440 | tf_op jit(solution)/shard_map/ppermute | solution.py:56
  (276 other events, 2549.5 us)
Sparse Core Ops, SparseCore 0:
  332.3 29.9 reduce-scatter.4
  379.6 30.4 reduce-scatter.6
  448.3 28.7 reduce-scatter.10
  485.4 29.5 reduce-scatter.8
